TPU v7x, 1024 devices: a whole 8x8x8 slice. The times are simulated.
1024 devices in a mesh: rows: 32 (over y_hi, z), cols: 32 (over y_lo, x, core).
Axes of the slice: x: 8, y: 8 (y_hi: 4, y_lo: 2; y = y_hi * 2 + y_lo), z: 8, core: 2. Of those that a mesh axis runs over, the one named last changes fastest.
Arguments:
- blocks: bfloat16 [512, 64, 128, 128], P('rows', 'cols'), may hold values from -0.5 to 0.5
- columns: int32 [512, 64], P('rows', 'cols'), may hold values from 0 to 511, as said below
- counts: int32 [512, 32], P('rows', 'cols'), may hold values from 1 to 2, as said below
- aggregate: int32 [512], replicated, may hold values from 0 to 63, as said below
- panels: bfloat16 [512, 24, 128], P('rows'), may hold values from -2.390625 to 2.390625
Outputs:
- coarse_band: float32 [64, 24, 1584], P('rows')
Inputs may be any that keep to these rules, and one draw needn't show every extreme that they name: `columns`: the block column of a slot of block row i lies in the range of block rows (i // 16 + d) * 16 to (i // 16 + d + 1) * 16 - 1 for some d with |d| <= 16. Slots c * 2 to c * 2 + 1 of a block row form group c; slot c * 2 + j holds a block if and only if j < counts[i, c]. Some group has all 2 slots live. `aggregate`: the 16 block rows from r * 16 belong to aggregates r * 2 to r * 2 + 1, exactly 8 to each.
All inputs are finite; a program needn't handle non-finite values.
Results may differ from a plain program's by a relative error of at most 0.0029.
Values may be sent and summed in bfloat16 or wider, within the bound.
No kernel may reach another device: no remote copies, remote signals or barrier semaphores. Data moves between devices by JAX's collectives and lax.ppermute only.
A program may use at most 32 MiB of HBM per device.

v0:
```python
import jax
import jax.numpy as jnp
from jax import lax
from jax.sharding import PartitionSpec as P

AGG_DEV = 2


def local(blocks, columns, counts, aggregate, panels):
    rows_here = panels.shape[0]
    modes_here = panels.shape[1]
    dofs_here = panels.shape[2]
    slots_here = blocks.shape[1]
    reach_rows = lax.axis_size("rows") // 2
    window_aggs = (2 * reach_rows + 1) * AGG_DEV
    row_index = lax.axis_index("rows")
    window = lax.all_gather(panels, "rows", axis=0, tiled=True)
    local_index = columns.reshape(-1)
    remote_panels = jnp.take(window, local_index, axis=0).reshape(
        rows_here, slots_here, modes_here, dofs_here
    )
    product = jnp.einsum(
        "iskl,isnl->isnk", blocks, remote_panels, preferred_element_type=jnp.float32
    ).astype(jnp.bfloat16)
    triple = jnp.einsum("imk,isnk->ismn", panels, product, preferred_element_type=jnp.float32)
    slot_within = jnp.arange(slots_here, dtype=jnp.int32)
    live_mask = (slot_within[None, :] < counts).astype(jnp.float32)
    weighted = triple * live_mask[:, :, None, None]
    window_agg = (
        jnp.take(aggregate, columns.reshape(-1), axis=0).reshape(rows_here, slots_here)
        - (row_index - reach_rows) * AGG_DEV
    )
    column_hot = (
        window_agg[:, :, None] == jnp.arange(window_aggs, dtype=jnp.int32)[None, None, :]
    ).astype(jnp.float32)
    own_aggs = (
        lax.dynamic_slice_in_dim(aggregate, row_index * rows_here, rows_here, 0)
        - row_index * AGG_DEV
    )
    row_hot = (own_aggs[:, None] == jnp.arange(AGG_DEV, dtype=jnp.int32)[None, :]).astype(
        jnp.float32
    )
    gathered = jnp.einsum("isb,ismn->imbn", column_hot, weighted, precision=lax.Precision.HIGHEST)
    coarse = jnp.einsum("ia,imbn->ambn", row_hot, gathered, precision=lax.Precision.HIGHEST)
    coarse = coarse.reshape(AGG_DEV, modes_here, window_aggs * modes_here)
    return lax.psum(coarse, "cols")


def solution(mesh):
    return jax.shard_map(
        local,
        mesh=mesh,
        in_specs=(
            P("rows", "cols", None, None),
            P("rows", "cols"),
            P("rows", "cols"),
            P(),
            P("rows", None, None),
        ),
        out_specs=P("rows", None, None),
        check_vma=False,
    )
```

profile of v0, /device:TPU:1, one launch (start us, length us, event | category | flops | bytes accessed | tf_op | source)
XLA Modules:
  0.0 360.8 jit_solution(9215915902461287032)
XLA Ops:
  6.5 0.0 copy-start
  6.5 0.0 all-gather.2.cloned.1.call-start
  6.5 0.7 all-gather.2.cloned.1.call-update
  7.3 0.0 all-reduce.2.cloned.1.call-start
  7.3 0.8 copy.29
  8.1 0.1 reshape.71
  8.2 1.4 gather_fusion.1
  9.6 0.1 gather.15
  9.7 0.1 copy.30
  9.7 0.7 select_subtract_fusion
  10.4 0.1 copy.28
  10.5 0.1 copy.31
  10.6 0.8 dynamic-slice_subtract_fusion
  11.4 0.7 fusion.14
  12.1 111.1 %all-gather.2.cloned.1.call-done = bf16[512,24,128]{2,1,0:T(8,128)(2,1)} async-done(((bf16[16,24,128]{2,1,0:T(8,128)(2,1)}), bf16[512,24,128]{2,1,0:T(8,128)(2,1)}) %all-gather.2.cloned.1.call-update) | async-done | bytes 3145744 | tf_op jit(solution)/shard_map/all_gather | solution.py:17
  123.2 2.5 gather_fusion
  125.7 0.0 copy-done
  125.7 1.8 fusion.2
  127.5 0.2 copy.32
  127.7 4.0 %convolution_bitcast_fusion = f32[16,24,66,24]{2,3,1,0:T(8,128)S(1)} fusion(f32[16,2,24,24]{3,1,2,0:T(2,128)S(1)} %copy.32, s32[16,2]{1,0:T(8,128)S(1)} %copy.31), kind=kOutput, calls=%fused_computation.4 | convolution fusion | flops 14600256 | bytes 2506880 | tf_op jit(solution)/shard_map/isb,ismn->imbn/dot_general | solution.py:43
  131.7 4.3 %fusion = f32[2,24,66,24]{2,0,3,1:T(2,128)S(1)} fusion(f32[16,24,66,24]{2,3,1,0:T(8,128)S(1)} %convolution_bitcast_fusion, s32[16]{0:T(128)S(1)} %dynamic-slice_subtract_fusion), kind=kOutput, calls=%fused_computation.2 | convolution fusion | flops 14598176 | bytes 2737216 | tf_op jit(solution)/shard_map/ia,imbn->ambn/dot_general | solution.py:44
  136.0 0.8 copy.34
  136.8 1.2 reshape.72
  138.0 0.0 all-reduce.2.cloned.1.call-update
  138.0 214.2 %all-reduce.2.cloned.1.call-done = f32[2,24,1584]{2,1,0:T(8,128)} async-done(((f32[2,24,1584]{2,1,0:T(8,128)}), f32[2,24,1584]{2,1,0:T(8,128)}) %all-reduce.2.cloned.1.call-update) | async-done | bytes 304144 | tf_op jit(solution)/shard_map/psum | solution.py:46
  352.3 1.7 copy.41
  (2 shorter events, 0.0 us)
Async XLA Ops:
  6.5 119.2 %copy-start = (bf16[16,2,128,128]{3,2,1,0:T(8,128)(2,1)S(1)}, bf16[16,2,128,128]{3,2,1,0:T(8,128)(2,1)}, u32[]{:S(2)}) copy-start(bf16[16,2,128,128]{3,2,1,0:T(8,128)(2,1)} %param.5) | copy-start | bytes 3145732
  6.5 116.7 %all-gather.2.cloned.1.call-start = ((), (), s32[]{:S(2)}) async-start(), calls=%async_computation | async-start | bytes 3244032 | tf_op jit(solution)/shard_map/all_gather | solution.py:17
  7.3 345.0 %all-reduce.2.cloned.1.call-start = ((), (), s32[]{:S(2)}) async-start(), calls=%async_computation.1 | async-start | bytes 638976 | tf_op jit(solution)/shard_map/psum | solution.py:46
Sparse Core Ops, SparseCore 0:
  11.7 111.4 all-gather.1
  138.1 214.0 all-reduce.1
where the time goes:
time: 361 us
  waiting for transfers between devices  326 us (90%)
  between operations  13.5 us (4%)
  matrix products  10.1 us (3%)
  local copies, waits for them, and re-layouts  8.99 us (2%)
    psum x1, waiting for transfers between devices, local(): return lax.psum(coarse, 'cols')  214 us
    all_gather x1, waiting for transfers between devices, local(): window = lax.all_gather(panels, 'rows', axis=0, tiled=True)  111 us
  transfers between devices with their start and end apart: 2, of which 2 were waited for; matrix products, arithmetic and copies ran while one was open for 1% of the time, Pallas kernels for 0%

commit v1 on v0

v1 whole, which is shorter than its diff:
```python
import jax
import jax.numpy as jnp
import numpy as np
from jax import lax
from jax.experimental import pallas as pl
from jax.experimental.pallas import tpu as pltpu
from jax.sharding import Mesh
from jax.sharding import PartitionSpec as P

AXES = ("yh", "z", "yl", "xh", "xl", "k")
SIZES = (4, 8, 2, 4, 2, 2)
ROWS = ("yh", "z")
COLS = ("yl", "xh", "xl", "k")
SHARE = ("yl", "xl", "k")
QUAD = ("yl", "xl")

ROWS_HERE = 16
SLOTS = 32
MODES = 24
DOFS = 128
AGG_DEV = 2
PAIR = AGG_DEV * MODES
CODES = AGG_DEV * 4 * ROWS_HERE
PLANES = MODES + 1
WIN = 1584
LIMIT = 24 * 1024 * 1024


def left_kernel(blocks, columns, counts, aggregate, panels, out, wide):
    row = lax.axis_index("yh") * 8 + lax.axis_index("z")
    lane = lax.broadcasted_iota(jnp.int32, (1, DOFS), 1)
    for i in range(ROWS_HERE):
        both = jnp.concatenate([blocks[i, 0], blocks[i, 1]], axis=1)
        left = jnp.dot(panels[i], both, preferred_element_type=jnp.float32)
        count = counts[i, 0]
        own = aggregate[row * ROWS_HERE + i] - row * AGG_DEV
        for s in range(2):
            slot = 2 * i + s
            wide[pl.ds(slot, MODES, stride=SLOTS), :] = left[:, s * DOFS : (s + 1) * DOFS]
            column = columns[i, s]
            code = own * 64 + (column >> 7) * 16 + (column & 15)
            code = jnp.where(s < count, code, -1)
            depth = ((column >> 4) & 7).astype(jnp.float32)
            wide[pl.ds(MODES * SLOTS + slot, 1), :] = jnp.where(lane == code, depth, -1.0)
    total = wide[...].astype(jnp.bfloat16)
    for u in range(4):
        out[u] = total


def middle_kernel(near, far, panels, aggregate, out, wide):
    q = lax.axis_index("yl") * 4 + lax.axis_index("xl") * 2 + lax.axis_index("k")

    def plane(m):
        parts = [ref[u, m * SLOTS : (m + 1) * SLOTS, :] for ref in (near, far) for u in range(4)]
        return jnp.concatenate(parts, axis=0)

    codes = plane(MODES).astype(jnp.float32)
    hot = (jnp.transpose(codes) == q.astype(jnp.float32)).astype(jnp.float32).astype(jnp.bfloat16)
    for m in range(0, MODES, 2):
        pair = jnp.concatenate([plane(m), plane(m + 1)], axis=1)
        summed = jnp.dot(hot, pair, preferred_element_type=jnp.float32)
        wide[m * CODES : (m + 1) * CODES, :] = summed[:, :DOFS]
        wide[(m + 1) * CODES : (m + 2) * CODES, :] = summed[:, DOFS:]
    found = []
    for y in range(4):
        group = y * 8 + q
        lefts, rights = [], []
        for j in range(ROWS_HERE):
            a0 = wide[pl.ds(y * 16 + j, MODES, stride=CODES), :]
            a1 = wide[pl.ds(64 + y * 16 + j, MODES, stride=CODES), :]
            lefts.append(jnp.concatenate([a0, a1], axis=0))
            which = aggregate[group * ROWS_HERE + j] - group * AGG_DEV
            panel = panels[y, j].astype(jnp.float32)
            zero = jnp.zeros_like(panel)
            halves = [jnp.where(which == b, panel, zero) for b in range(AGG_DEV)]
            rights.append(jnp.concatenate(halves, axis=0).astype(jnp.bfloat16))
        left = jnp.concatenate(lefts, axis=1)
        high = left.astype(jnp.bfloat16)
        low = (left - high.astype(jnp.float32)).astype(jnp.bfloat16)
        right = jnp.concatenate(rights, axis=1)
        over = (((1,), (1,)), ((), ()))
        found.append(
            lax.dot_general(high, right, over, preferred_element_type=jnp.float32)
            + lax.dot_general(low, right, over, preferred_element_type=jnp.float32)
        )
    row = jnp.concatenate(found, axis=1)
    first = row[:, :128]
    rest = jnp.concatenate([row[:MODES, 128:], row[MODES:, 128:]], axis=1)
    for u in range(4):
        out[u, :PAIR, :] = first
        out[u, PAIR:, :] = rest


def place_kernel(parts, out, wide):
    row = lax.axis_index("yh") * 8 + lax.axis_index("z")
    lane = lax.broadcasted_iota(jnp.int32, (PAIR, 256), 1)
    windows = [jnp.zeros((PAIR, 256), jnp.float32) for _ in range(6)]
    for q in range(8):
        rest = parts[q, PAIR:, :]
        tail = jnp.concatenate([rest, pltpu.roll(rest, 64, axis=1)], axis=0)
        source = jnp.concatenate([parts[q, :PAIR, :], tail], axis=1)
        for y in range(4):
            start = (y * 8 + q) * PAIR
            at = start % 256
            turned = pltpu.roll(source, (start - y * PAIR) % 256, axis=1)
            w = start // 256
            windows[w] = jnp.where((lane >= at) & (lane < at + PAIR), turned, windows[w])
            if at + PAIR > 256:
                windows[w + 1] = jnp.where(lane < at + PAIR - 256, turned, windows[w + 1])
    wide[:, : 6 * 128] = jnp.zeros((PAIR, 6 * 128), jnp.float32)
    wide[:, 18 * 128 :] = jnp.zeros((PAIR, 7 * 128), jnp.float32)
    for w in range(6):
        wide[:, (6 + 2 * w) * 128 : (8 + 2 * w) * 128] = windows[w]
    offset = row * PAIR
    base = pl.multiple_of((offset // 128) * 128, 128)
    shift = offset % 128
    narrow = lax.broadcasted_iota(jnp.int32, (PAIR, 128), 1)
    turned = []
    for t in range(14):
        tile = wide[:, pl.ds(base + t * 128, 128)]
        turned.append(pltpu.roll(tile, (128 - shift) % 128, axis=1))
    for t in range(13):
        tile = jnp.where(narrow < 128 - shift, turned[t], turned[t + 1])
        width = min(128, WIN - t * 128)
        for a in range(AGG_DEV):
            out[a, :, t * 128 : t * 128 + width] = tile[a * MODES : (a + 1) * MODES, :width]


def everything(space, count):
    return [pl.BlockSpec(memory_space=space) for _ in range(count)]


VMEM, SMEM = pltpu.VMEM, pltpu.SMEM


def local(blocks, columns, counts, aggregate, panels):
    f32, bf16 = jnp.float32, jnp.bfloat16
    params = pltpu.CompilerParams(vmem_limit_bytes=LIMIT)

    pairs = []
    for yh, z, yl, xh, xl, k in np.ndindex(*SIZES):
        source = (yh, yl * 4 + xl * 2 + k, (z >> 2) & 1, xh, (z >> 1) & 1, z & 1)
        pairs.append(
            (int(np.ravel_multi_index(source, SIZES)), int(np.ravel_multi_index((yh, z, yl, xh, xl, k), SIZES)))
        )
    turned = lax.ppermute(panels, AXES, pairs)
    gathered = lax.all_to_all(
        jnp.broadcast_to(turned[None], (4,) + turned.shape), "yh", 0, 0, tiled=True
    )

    left = pl.pallas_call(
        left_kernel,
        out_shape=jax.ShapeDtypeStruct((4, PLANES * SLOTS, DOFS), bf16),
        in_specs=[
            pl.BlockSpec(memory_space=VMEM),
            pl.BlockSpec(memory_space=SMEM),
            pl.BlockSpec(memory_space=SMEM),
            pl.BlockSpec(memory_space=SMEM),
            pl.BlockSpec(memory_space=VMEM),
        ],
        out_specs=pl.BlockSpec(memory_space=VMEM),
        scratch_shapes=[pltpu.VMEM((PLANES * SLOTS, DOFS), f32)],
        compiler_params=params,
        cost_estimate=pl.CostEstimate(flops=25_000_000, bytes_accessed=2_000_000, transcendentals=0),
        name="left",
    )(blocks, columns, counts, aggregate, panels)
    near = lax.all_to_all(left, QUAD, 0, 0, tiled=True)
    far = lax.ppermute(near, "k", [(0, 1), (1, 0)])

    part = pl.pallas_call(
        middle_kernel,
        out_shape=jax.ShapeDtypeStruct((4, PAIR + MODES, DOFS), f32),
        in_specs=[
            pl.BlockSpec(memory_space=VMEM),
            pl.BlockSpec(memory_space=VMEM),
            pl.BlockSpec(memory_space=VMEM),
            pl.BlockSpec(memory_space=SMEM),
        ],
        out_specs=pl.BlockSpec(memory_space=VMEM),
        scratch_shapes=[pltpu.VMEM((MODES * CODES, DOFS), f32)],
        compiler_params=params,
        cost_estimate=pl.CostEstimate(flops=500_000_000, bytes_accessed=3_000_000, transcendentals=0),
        name="middle",
    )(near, far, gathered, aggregate)

    shares = lax.all_to_all(part, "xh", 0, 0, tiled=True)
    whole = jnp.sum(shares, axis=0)
    spread = lax.all_to_all(
        jnp.broadcast_to(whole[None], (8,) + whole.shape), SHARE, 0, 0, tiled=True
    )
    return pl.pallas_call(
        place_kernel,
        out_shape=jax.ShapeDtypeStruct((AGG_DEV, MODES, WIN), f32),
        in_specs=[pl.BlockSpec(memory_space=VMEM)],
        out_specs=pl.BlockSpec(memory_space=VMEM),
        scratch_shapes=[pltpu.VMEM((PAIR, 25 * 128), f32)],
        compiler_params=params,
        cost_estimate=pl.CostEstimate(flops=1_000_000, bytes_accessed=600_000, transcendentals=0),
        name="place",
    )(spread)


def solution(mesh):
    inner = Mesh(mesh.devices.reshape(SIZES), AXES)
    return jax.shard_map(
        local,
        mesh=inner,
        in_specs=(
            P(ROWS, COLS, None, None),
            P(ROWS, COLS),
            P(ROWS, COLS),
            P(),
            P(ROWS, None, None),
        ),
        out_specs=P(ROWS, None, None),
        check_vma=False,
    )
```

time: 361 us -> 94.9 us (0.26)
  waiting for transfers between devices: 326 us -> 4.01 us
  blocking collectives: 0 us -> 64.2 us
  starting transfers between devices: 0.04 us -> 17.3 us
  between operations: 13.5 us -> 0.05 us
  matrix products: 10.1 us -> 0 us
  local copies, waits for them, and re-layouts: 8.99 us -> 3.64 us
  Pallas kernels: 0 us -> 5.31 us
    psum x1 -> x0, waiting for transfers between devices: 214 us -> none  [local(): return lax.psum(coarse, 'cols')]
    all_gather x1 -> x0, waiting for transfers between devices: 111 us -> none  [local(): window = lax.all_gather(panels, 'rows', axis=0, tiled=True)]
    all_to_all x0 -> x4, blocking collectives: none -> 64.2 us  [the longest x1 30.1 us: local(): lax.all_to_all(jnp.broadcast_to(whole[None], (8,) + whole.shape), SHARE,...]
    ppermute x0 -> x2, starting transfers between devices: none -> 17.3 us  [the longest x1 15.4 us: local(): far = lax.ppermute(near, 'k', [(0, 1), (1, 0)])]
    dot_general x3 -> x0, matrix products: 10.1 us -> none  [the longest x1 4.34 us: local(): jnp.einsum('ia,imbn->ambn', row_hot, gathered, precision=lax.Precision.HI...]
    pallas_call x0 -> x3, Pallas kernels: none -> 5.31 us  [the longest x1 2.35 us: local(): pl.pallas_call(middle_kernel, out_shape=jax.ShapeDtypeStruct((4, PAIR + M...]
    gather x4 -> x0, local copies, waits for them, and re-layouts: 4.05 us -> none  [the longest x1 2.49 us: local(): jnp.take(window, local_index, axis=0)]
    ppermute x0 -> x2, waiting for transfers between devices: none -> 4.01 us  [the longest x1 4.01 us: local(): turned = lax.ppermute(panels, AXES, pairs)]
  transfers between devices with their start and end apart: 2 -> 2, of which waited for: 2 -> 1; matrix products, arithmetic and copies ran while one was open for 1% -> 0% of each run, Pallas kernels for 0% -> 0%
where the time goes in v1:
time: 94.9 us; the launch traced here: 94.5 us
  blocking collectives  64.2 us (68%)
  starting transfers between devices  17.3 us (18%)
  Pallas kernels  5.31 us (6%)
  waiting for transfers between devices  4.01 us (4%)
  local copies, waits for them, and re-layouts  3.64 us (4%)
    all_to_all x1, blocking collectives, local(): lax.all_to_all(jnp.broadcast_to(whole[None], (8,) + whole.shape), SHARE,...  30.1 us
    ppermute x1, starting transfers between devices, local(): far = lax.ppermute(near, 'k', [(0, 1), (1, 0)])  15.4 us
    all_to_all x1, blocking collectives, local(): near = lax.all_to_all(left, QUAD, 0, 0, tiled=True)  12.1 us
    all_to_all x1, blocking collectives, local(): lax.all_to_all(jnp.broadcast_to(turned[None], (4,) + turned.shape), 'yh',...  11.7 us
    all_to_all x1, blocking collectives, local(): shares = lax.all_to_all(part, 'xh', 0, 0, tiled=True)  10.4 us
    ppermute x1, waiting for transfers between devices, local(): turned = lax.ppermute(panels, AXES, pairs)  4.01 us
    unnamed x10, local copies, waits for them, and re-layouts  3.57 us
    pallas_call x1, Pallas kernels, local(): pl.pallas_call(middle_kernel, out_shape=jax.ShapeDtypeStruct((4, PAIR + M...  2.35 us
  transfers between devices with their start and end apart: 2, of which 1 were waited for; matrix products, arithmetic and copies ran while one was open for 0% of the time, Pallas kernels for 0%

profile of v1, /device:TPU:1, one launch (start us, length us, event | category | flops | bytes accessed | tf_op | source)
XLA Modules:
  0.0 94.5 jit_solution(108144104087371752)
XLA Ops:
  0.0 0.0 copy-start.3
  0.0 0.8 copy.6.columns
  0.8 0.0 copy-done.3
  0.8 0.0 copy-start.2
  0.8 0.1 copy.7.counts
  0.9 0.6 copy-done.2
  1.5 0.0 copy-start
  1.5 1.2 %copy-done = bf16[16,2,128,128]{3,2,1,0:T(8,128)(2,1)S(1)} copy-done((bf16[16,2,128,128]{3,2,1,0:T(8,128)(2,1)S(1)}, bf16[16,2,128,128]{3,2,1,0:T(8,128)(2,1)}, u32[]{:S(2)}) %copy-start) | copy-done | bytes 1048600
  2.7 0.0 copy-start.1
  2.7 0.9 copy-done.1
  3.6 1.3 %left.1 = bf16[4,800,128]{2,1,0:T(8,128)(2,1)S(1)} custom-call(bf16[16,2,128,128]{3,2,1,0:T(8,128)(2,1)S(1)} %copy-done, s32[16,2]{1,0:T(8,128)S(1)} %copy.6.columns, s32[16,1]{1,0:T(8,128)S(1)} %copy.7.counts, s32[512]{0:T(512)S(1)} %copy-done.2, bf16[16,24,128]{2,1,0:T(8,128)(2,1)S(1)} %copy-done.1), custom_call_target="tpu_custom_call" | custom-call | flops 25000000 | bytes 2000000 | tf_op jit(solution)/shard_map/left/pallas_call | solution.py:151
  4.9 12.1 %all_to_all.20.near = bf16[4,800,128]{2,1,0:T(8,128)(2,1)S(1)} all-to-all(bf16[4,800,128]{2,1,0:T(8,128)(2,1)S(1)} %left.1), channel_id=1, replica_groups=mesh['yh'=4,'z'=8,'yl'=2,'xh'=4,'xl'=2,'k'=2] {'yl','xl'}, dimensions={0} | all-to-all | bytes 1638400 | tf_op jit(solution)/shard_map/all_to_all | solution.py:167
  16.9 15.4 %collective-permute-start = (bf16[4,800,128]{2,1,0:T(8,128)(2,1)S(1)}, bf16[4,800,128]{2,1,0:T(8,128)(2,1)S(1)}, u32[]{:S(2)}, u32[]{:S(2)}) collective-permute-start(bf16[4,800,128]{2,1,0:T(8,128)(2,1)S(1)} %all_to_all.20.near), channel_id=1, source_target_pairs={{0,1},{1,0},{2,3},{3,2},{4,5},{5,4},{6,7},{7,6},{8,9},{9,8},{10,11... | collective-permute-start | bytes 2457608 | tf_op jit(solution)/shard_map/ppermute | solution.py:168
  32.3 1.9 %collective-permute-start.1 = (bf16[16,24,128]{2,1,0:T(8,128)(2,1)S(1)}, bf16[16,24,128]{2,1,0:T(8,128)(2,1)S(1)}, u32[]{:S(2)}, u32[]{:S(2)}) collective-permute-start(bf16[16,24,128]{2,1,0:T(8,128)(2,1)S(1)} %copy-done.1), channel_id=1, source_target_pairs={{0,0},{32,1},{64,2},{96,3},{4,4},{36,5},{68,6},{100,7},{8,8},{40,9... | collective-permute-start | bytes 294920 | tf_op jit(solution)/shard_map/ppermute | solution.py:146
  34.2 4.0 %collective-permute-done.1 = bf16[16,24,128]{2,1,0:T(8,128)(2,1)S(1)} collective-permute-done((bf16[16,24,128]{2,1,0:T(8,128)(2,1)S(1)}, bf16[16,24,128]{2,1,0:T(8,128)(2,1)S(1)}, u32[]{:S(2)}, u32[]{:S(2)}) %collective-permute-start.1) | collective-permute-done | bytes 98336 | tf_op jit(solution)/shard_map/ppermute | solution.py:146
  38.2 0.1 broadcast_in_dim.4
  38.3 11.7 %all_to_all.21.panels = bf16[4,16,24,128]{3,2,1,0:T(8,128)(2,1)S(1)} all-to-all(bf16[4,16,24,128]{3,2,1,0:T(8,128)(2,1)S(1)} %broadcast_in_dim.4), channel_id=1, replica_groups=mesh['yh'=4,'z'=8,'yl'=2,'xh'=4,'xl'=2,'k'=2] {'yh'}, dimensions={0} | all-to-all | bytes 786432 | tf_op jit(solution)/shard_map/all_to_all | solution.py:147
  50.0 0.0 collective-permute-done.far
  50.0 2.3 %middle.1 = f32[4,72,128]{2,1,0:T(8,128)S(1)} custom-call(bf16[4,800,128]{2,1,0:T(8,128)(2,1)S(1)} %all_to_all.20.near, bf16[4,800,128]{2,1,0:T(8,128)(2,1)S(1)} %collective-permute-done.far, bf16[4,16,24,128]{3,2,1,0:T(8,128)(2,1)S(1)} %all_to_all.21.panels, s32[512]{0:T(512)S(1)} %copy-done.2), custom_call_target="tpu_custom_call" | custom-call | flops 500000000 | bytes 3000000 | tf_op jit(solution)/shard_map/middle/pallas_call | solution.py:170
  52.4 10.4 %all_to_all.22 = f32[4,72,128]{2,1,0:T(8,128)S(1)} all-to-all(f32[4,72,128]{2,1,0:T(8,128)S(1)} %middle.1), channel_id=1, replica_groups=mesh['yh'=4,'z'=8,'yl'=2,'xh'=4,'xl'=2,'k'=2] {'xh'}, dimensions={0} | all-to-all | bytes 294912 | tf_op jit(solution)/shard_map/all_to_all | solution.py:186
  62.8 30.1 %all_to_all.23.parts = f32[8,72,128]{2,1,0:T(8,128)S(1)} all-to-all(f32[8,72,128]{2,1,0:T(8,128)S(1)} %broadcast_in_dim.5), channel_id=1, replica_groups=mesh['yh'=4,'z'=8,'yl'=2,'xh'=4,'xl'=2,'k'=2] {'yl','xl','k'}, dimensions={0} | all-to-all | bytes 589824 | tf_op jit(solution)/shard_map/all_to_all | solution.py:188
  92.9 1.7 %place.1 = f32[2,24,1584]{2,1,0:T(8,128)} custom-call(f32[8,72,128]{2,1,0:T(8,128)S(1)} %all_to_all.23.parts), custom_call_target="tpu_custom_call" | custom-call | flops 1000000 | bytes 600000 | tf_op jit(solution)/shard_map/place/pallas_call | solution.py:191
  (2 shorter events, 0.0 us)
Async XLA Ops:
  0.0 0.8 copy-start.3
  0.8 0.7 copy-start.2
  1.5 1.2 %copy-start = (bf16[16,2,128,128]{3,2,1,0:T(8,128)(2,1)S(1)}, bf16[16,2,128,128]{3,2,1,0:T(8,128)(2,1)}, u32[]{:S(2)}) copy-start(bf16[16,2,128,128]{3,2,1,0:T(8,128)(2,1)} %blocks.1) | copy-start | bytes 3145732
  2.7 0.9 copy-start.1
  16.9 33.1 %collective-permute-start = (bf16[4,800,128]{2,1,0:T(8,128)(2,1)S(1)}, bf16[4,800,128]{2,1,0:T(8,128)(2,1)S(1)}, u32[]{:S(2)}, u32[]{:S(2)}) collective-permute-start(bf16[4,800,128]{2,1,0:T(8,128)(2,1)S(1)} %all_to_all.20.near), channel_id=1, source_target_pairs={{0,1},{1,0},{2,3},{3,2},{4,5},{5,4},{6,7},{7,6},{8,9},{9,8},{10,11... | collective-permute-start | bytes 2457608 | tf_op jit(solution)/shard_map/ppermute | solution.py:168
  32.3 5.9 %collective-permute-start.1 = (bf16[16,24,128]{2,1,0:T(8,128)(2,1)S(1)}, bf16[16,24,128]{2,1,0:T(8,128)(2,1)S(1)}, u32[]{:S(2)}, u32[]{:S(2)}) collective-permute-start(bf16[16,24,128]{2,1,0:T(8,128)(2,1)S(1)} %copy-done.1), channel_id=1, source_target_pairs={{0,0},{32,1},{64,2},{96,3},{4,4},{36,5},{68,6},{100,7},{8,8},{40,9... | collective-permute-start | bytes 294920 | tf_op jit(solution)/shard_map/ppermute | solution.py:146

commit v2 on v1

--- a/solution.py
+++ b/solution.py
@@ -7,9 +7,9 @@
 from jax.sharding import Mesh
 from jax.sharding import PartitionSpec as P
 
-AXES = ("yh", "z", "yl", "xh", "xl", "k")
-SIZES = (4, 8, 2, 4, 2, 2)
-ROWS = ("yh", "z")
+AXES = ("yh", "zh", "zl", "yl", "xh", "xl", "k")
+SIZES = (4, 4, 2, 2, 4, 2, 2)
+ROWS = ("yh", "zh", "zl")
 COLS = ("yl", "xh", "xl", "k")
 SHARE = ("yl", "xl", "k")
 QUAD = ("yl", "xl")
@@ -24,30 +24,51 @@
 PLANES = MODES + 1
 WIN = 1584
 LIMIT = 24 * 1024 * 1024
-
-
-def left_kernel(blocks, columns, counts, aggregate, panels, out, wide):
-    row = lax.axis_index("yh") * 8 + lax.axis_index("z")
+FULL = 63 * 1024 * 1024
+
+
+def left_kernel(*refs):
+    far = refs[:5]
+    out, wide, blocks, columns, counts, aggregate, panels, arrived = refs[5:]
+    pieces = 4
+    step = ROWS_HERE // pieces
+    copies = [
+        pltpu.make_async_copy(far[n], here, arrived.at[n])
+        for n, here in ((1, columns), (2, counts), (3, aggregate), (4, panels))
+    ]
+    for p in range(pieces):
+        part = pl.ds(p * step, step)
+        copies.append(pltpu.make_async_copy(far[0].at[part], blocks.at[part], arrived.at[5 + p]))
+    for copy in copies:
+        copy.start()
+    for copy in copies[:3]:
+        copy.wait()
+    row = lax.axis_index("yh") * 8 + lax.axis_index("zh") * 2 + lax.axis_index("zl")
     lane = lax.broadcasted_iota(jnp.int32, (1, DOFS), 1)
     for i in range(ROWS_HERE):
+        count = counts[0, i]
+        own = aggregate[row * ROWS_HERE + i] - row * AGG_DEV
+        for s in range(2):
+            column = columns[s, i]
+            code = own * 64 + ((column >> 5) & 3) * 16 + (column & 15)
+            code = jnp.where(s < count, code, -1)
+            place = ((column >> 7) * 2 + ((column >> 4) & 1)).astype(jnp.float32)
+            at = MODES * SLOTS + 2 * i + s
+            wide[pl.ds(at, 1), :] = jnp.where(lane == code, place, -1.0)
+    copies[3].wait()
+    for i in range(ROWS_HERE):
+        if i % step == 0:
+            copies[4 + i // step].wait()
         both = jnp.concatenate([blocks[i, 0], blocks[i, 1]], axis=1)
         left = jnp.dot(panels[i], both, preferred_element_type=jnp.float32)
-        count = counts[i, 0]
-        own = aggregate[row * ROWS_HERE + i] - row * AGG_DEV
         for s in range(2):
-            slot = 2 * i + s
-            wide[pl.ds(slot, MODES, stride=SLOTS), :] = left[:, s * DOFS : (s + 1) * DOFS]
-            column = columns[i, s]
-            code = own * 64 + (column >> 7) * 16 + (column & 15)
-            code = jnp.where(s < count, code, -1)
-            depth = ((column >> 4) & 7).astype(jnp.float32)
-            wide[pl.ds(MODES * SLOTS + slot, 1), :] = jnp.where(lane == code, depth, -1.0)
-    total = wide[...].astype(jnp.bfloat16)
-    for u in range(4):
-        out[u] = total
-
-
-def middle_kernel(near, far, panels, aggregate, out, wide):
+            wide[pl.ds(2 * i + s, MODES, stride=SLOTS), :] = left[:, s * DOFS : (s + 1) * DOFS]
+    out[...] = wide[...].astype(jnp.bfloat16)
+
+
+def middle_kernel(near, far, panels, aggregate_far, out, wide, aggregate, arrived):
+    copy = pltpu.make_async_copy(aggregate_far, aggregate, arrived)
+    copy.start()
     q = lax.axis_index("yl") * 4 + lax.axis_index("xl") * 2 + lax.axis_index("k")
 
     def plane(m):
@@ -61,9 +82,10 @@
         summed = jnp.dot(hot, pair, preferred_element_type=jnp.float32)
         wide[m * CODES : (m + 1) * CODES, :] = summed[:, :DOFS]
         wide[(m + 1) * CODES : (m + 2) * CODES, :] = summed[:, DOFS:]
+    copy.wait()
     found = []
     for y in range(4):
-        group = y * 8 + q
+        group = (q >> 1) * 8 + y * 2 + (q & 1)
         lefts, rights = [], []
         for j in range(ROWS_HERE):
             a0 = wide[pl.ds(y * 16 + j, MODES, stride=CODES), :]
@@ -92,7 +114,7 @@
 
 
 def place_kernel(parts, out, wide):
-    row = lax.axis_index("yh") * 8 + lax.axis_index("z")
+    row = lax.axis_index("yh") * 8 + lax.axis_index("zh") * 2 + lax.axis_index("zl")
     lane = lax.broadcasted_iota(jnp.int32, (PAIR, 256), 1)
     windows = [jnp.zeros((PAIR, 256), jnp.float32) for _ in range(6)]
     for q in range(8):
@@ -100,7 +122,7 @@
         tail = jnp.concatenate([rest, pltpu.roll(rest, 64, axis=1)], axis=0)
         source = jnp.concatenate([parts[q, :PAIR, :], tail], axis=1)
         for y in range(4):
-            start = (y * 8 + q) * PAIR
+            start = ((q >> 1) * 8 + y * 2 + (q & 1)) * PAIR
             at = start % 256
             turned = pltpu.roll(source, (start - y * PAIR) % 256, axis=1)
             w = start // 256
@@ -138,34 +160,42 @@
     params = pltpu.CompilerParams(vmem_limit_bytes=LIMIT)
 
     pairs = []
-    for yh, z, yl, xh, xl, k in np.ndindex(*SIZES):
-        source = (yh, yl * 4 + xl * 2 + k, (z >> 2) & 1, xh, (z >> 1) & 1, z & 1)
-        pairs.append(
-            (int(np.ravel_multi_index(source, SIZES)), int(np.ravel_multi_index((yh, z, yl, xh, xl, k), SIZES)))
-        )
+    for yh, zh, zl, yl, xh, xl, k in np.ndindex(*SIZES):
+        source = (yl * 2 + xl, zh, k, yh >> 1, xh, yh & 1, zl)
+        target = (yh, zh, zl, yl, xh, xl, k)
+        pairs.append(tuple(int(np.ravel_multi_index(at, SIZES)) for at in (source, target)))
     turned = lax.ppermute(panels, AXES, pairs)
-    gathered = lax.all_to_all(
-        jnp.broadcast_to(turned[None], (4,) + turned.shape), "yh", 0, 0, tiled=True
-    )
 
     left = pl.pallas_call(
         left_kernel,
-        out_shape=jax.ShapeDtypeStruct((4, PLANES * SLOTS, DOFS), bf16),
-        in_specs=[
-            pl.BlockSpec(memory_space=VMEM),
-            pl.BlockSpec(memory_space=SMEM),
-            pl.BlockSpec(memory_space=SMEM),
-            pl.BlockSpec(memory_space=SMEM),
-            pl.BlockSpec(memory_space=VMEM),
+        out_shape=jax.ShapeDtypeStruct((PLANES * SLOTS, DOFS), bf16),
+        in_specs=everything(pltpu.HBM, 5),
+        out_specs=pl.BlockSpec(memory_space=VMEM),
+        scratch_shapes=[
+            pltpu.VMEM((PLANES * SLOTS, DOFS), f32),
+            pltpu.VMEM(blocks.shape, bf16),
+            pltpu.SMEM((2, ROWS_HERE), jnp.int32),
+            pltpu.SMEM((1, ROWS_HERE), jnp.int32),
+            pltpu.SMEM(aggregate.shape, jnp.int32),
+            pltpu.VMEM(panels.shape, bf16),
+            pltpu.SemaphoreType.DMA((9,)),
         ],
-        out_specs=pl.BlockSpec(memory_space=VMEM),
-        scratch_shapes=[pltpu.VMEM((PLANES * SLOTS, DOFS), f32)],
-        compiler_params=params,
+        compiler_params=pltpu.CompilerParams(vmem_limit_bytes=FULL),
         cost_estimate=pl.CostEstimate(flops=25_000_000, bytes_accessed=2_000_000, transcendentals=0),
         name="left",
-    )(blocks, columns, counts, aggregate, panels)
-    near = lax.all_to_all(left, QUAD, 0, 0, tiled=True)
-    far = lax.ppermute(near, "k", [(0, 1), (1, 0)])
+    )(blocks, columns.T, counts.T, aggregate, panels)
+    left, turned = lax.optimization_barrier((left, turned))
+    swap = [(0, 1), (1, 0)]
+    cross = [(0, 3), (1, 2), (2, 1), (3, 0)]
+    beside = lax.ppermute(left, "xl", swap)
+    above = lax.ppermute(left, "yl", swap)
+    across = lax.ppermute(left, QUAD, cross)
+    gathered = lax.all_to_all(
+        jnp.broadcast_to(turned[None], (4,) + turned.shape), "zh", 0, 0, tiled=True
+    )
+    beside, above, across, gathered = lax.optimization_barrier((beside, above, across, gathered))
+    near = jnp.stack([left, beside, above, across])
+    far = lax.ppermute(near, "k", swap)
 
     part = pl.pallas_call(
         middle_kernel,
@@ -174,10 +204,14 @@
             pl.BlockSpec(memory_space=VMEM),
             pl.BlockSpec(memory_space=VMEM),
             pl.BlockSpec(memory_space=VMEM),
-            pl.BlockSpec(memory_space=SMEM),
+            pl.BlockSpec(memory_space=pltpu.HBM),
         ],
         out_specs=pl.BlockSpec(memory_space=VMEM),
-        scratch_shapes=[pltpu.VMEM((MODES * CODES, DOFS), f32)],
+        scratch_shapes=[
+            pltpu.VMEM((MODES * CODES, DOFS), f32),
+            pltpu.SMEM(aggregate.shape, jnp.int32),
+            pltpu.SemaphoreType.DMA,
+        ],
         compiler_params=params,
         cost_estimate=pl.CostEstimate(flops=500_000_000, bytes_accessed=3_000_000, transcendentals=0),
         name="middle",

time: 94.9 us -> 78.6 us (0.83)
  blocking collectives: 64.2 us -> 25.6 us
  starting transfers between devices: 17.3 us -> 38.1 us
  waiting for transfers between devices: 4.01 us -> 7.17 us
  local copies, waits for them, and re-layouts: 3.64 us -> 0.84 us
    all_to_all x2 -> x0, blocking collectives: 23.8 us -> none  [the longest x1 12.1 us: local(): near = lax.all_to_all(left, QUAD, 0, 0, tiled=True)]
    all_to_all x1, blocking collectives: 30.1 us -> 12.6 us  [local(): lax.all_to_all(jnp.broadcast_to(whole[None], (8,) + whole.shape), SHARE,...]
    all_to_all x0 -> x1, starting transfers between devices: none -> 14.7 us  [local(): lax.all_to_all(jnp.broadcast_to(turned[None], (4,) + turned.shape), 'zh',...]
    ppermute x1 -> x4, waiting for transfers between devices: 0.01 us -> 7.16 us  [the longest x1 3.67 us: local(): above = lax.ppermute(left, 'yl', swap)]
    ppermute x1, starting transfers between devices: 1.92 us -> 6.29 us  [local(): turned = lax.ppermute(panels, AXES, pairs)]
    ppermute x1, waiting for transfers between devices: 4.01 us -> 0.01 us  [local(): turned = lax.ppermute(panels, AXES, pairs)]
    unnamed x10 -> x4, local copies, waits for them, and re-layouts: 3.57 us -> 0.01 us
    all_to_all x1, blocking collectives: 10.4 us -> 13 us  [local(): shares = lax.all_to_all(part, 'xh', 0, 0, tiled=True)]
  transfers between devices with their start and end apart: 2 -> 6, of which waited for: 1 -> 3; matrix products, arithmetic and copies ran while one was open for 0% -> 0% of each run, Pallas kernels for 0% -> 3%
where the time goes in v2:
time: 78.6 us; the launch traced here: 78.1 us
  starting transfers between devices  38.1 us (48%)
  blocking collectives  25.6 us (33%)
  waiting for transfers between devices  7.17 us (9%)
  Pallas kernels  6.22 us (8%)
  local copies, waits for them, and re-layouts  0.84 us (1%)
    all_to_all x1, starting transfers between devices, local(): lax.all_to_all(jnp.broadcast_to(turned[None], (4,) + turned.shape), 'zh',...  14.7 us
    all_to_all x1, blocking collectives, local(): shares = lax.all_to_all(part, 'xh', 0, 0, tiled=True)  13 us
    all_to_all x1, blocking collectives, local(): lax.all_to_all(jnp.broadcast_to(whole[None], (8,) + whole.shape), SHARE,...  12.6 us
    ppermute x1, starting transfers between devices, local(): across = lax.ppermute(left, QUAD, cross)  9.24 us
    ppermute x1, starting transfers between devices, local(): turned = lax.ppermute(panels, AXES, pairs)  6.29 us
    ppermute x1, waiting for transfers between devices, local(): above = lax.ppermute(left, 'yl', swap)  3.67 us
    ppermute x1, starting transfers between devices, local(): beside = lax.ppermute(left, 'xl', swap)  3.09 us
    ppermute x1, starting transfers between devices, local(): above = lax.ppermute(left, 'yl', swap)  2.83 us
  transfers between devices with their start and end apart: 6, of which 3 were waited for; matrix products, arithmetic and copies ran while one was open for 0% of the time, Pallas kernels for 3%

profile of v2, /device:TPU:1, one launch (start us, length us, event | category | flops | bytes accessed | tf_op | source)
XLA Modules:
  0.0 78.1 jit_solution(16164213380535546876)
XLA Ops:
  0.0 6.3 %collective-permute-start = (bf16[16,24,128]{2,1,0:T(8,128)(2,1)}, bf16[16,24,128]{2,1,0:T(8,128)(2,1)S(1)}, u32[]{:S(2)}, u32[]{:S(2)}) collective-permute-start(bf16[16,24,128]{2,1,0:T(8,128)(2,1)} %refs_4_.1), channel_id=1, source_target_pairs={{0,0},{32,1},{256,2},{288,3},{4,4},{36,5},{260,6},{292,7},{8,8},{4... | collective-permute-start | bytes 294920 | tf_op jit(solution)/shard_map/ppermute | solution.py:167
  6.3 2.5 %left.1 = bf16[800,128]{1,0:T(8,128)(2,1)} custom-call(bf16[16,2,128,128]{3,2,1,0:T(8,128)(2,1)} %refs_0_.1, s32[2,16]{1,0:T(2,128)} %bitcast.10, s32[1,16]{1,0:T(1,128)} %bitcast.11, s32[512]{0:T(512)} %aggregate_far.1, bf16[16,24,128]{2,1,0:T(8,128)(2,1)} %refs_4_.1), custom_call_target="tpu_custom_call" | custom-call | flops 25000000 | bytes 2000000 | tf_op jit(solution)/shard_map/left/pallas_call | solution.py:169
  8.8 0.0 collective-permute-done
  8.8 0.8 %broadcast_in_dim.4 = bf16[4,16,24,128]{3,2,1,0:T(8,128)(2,1)} broadcast(bf16[16,24,128]{2,1,0:T(8,128)(2,1)S(1)} %collective-permute-done), dimensions={1,2,3} | broadcast | bytes 491520 | tf_op jit(solution)/shard_map/broadcast_in_dim | solution.py:194
  9.7 0.0 copy-start.1
  9.7 14.7 %all-to-all-start = ((bf16[4,16,24,128]{3,2,1,0:T(8,128)(2,1)}), bf16[4,16,24,128]{3,2,1,0:T(8,128)(2,1)S(1)}, u32[]{:S(2)}, u32[]{:S(2)}) async-start(bf16[4,16,24,128]{3,2,1,0:T(8,128)(2,1)} %broadcast_in_dim.4), calls=%async_computation | async-start | bytes 786432 | tf_op jit(solution)/shard_map/all_to_all | solution.py:193
  24.4 0.0 copy-done.1
  24.4 9.2 %collective-permute-start.3 = (bf16[800,128]{1,0:T(8,128)(2,1)S(1)}, bf16[800,128]{1,0:T(8,128)(2,1)S(1)}, u32[]{:S(2)}, u32[]{:S(2)}) collective-permute-start(bf16[800,128]{1,0:T(8,128)(2,1)S(1)} %copy-done.1), channel_id=1, source_target_pairs={{0,18},{2,16},{16,2},{18,0},{1,19},{3,17},{17,3},{19,1},{4,22},{6,... | collective-permute-start | bytes 614408 | tf_op jit(solution)/shard_map/ppermute | solution.py:192
  33.6 2.8 %collective-permute-start.2 = (bf16[800,128]{1,0:T(8,128)(2,1)S(1)}, bf16[800,128]{1,0:T(8,128)(2,1)S(1)}, u32[]{:S(2)}, u32[]{:S(2)}) collective-permute-start(bf16[800,128]{1,0:T(8,128)(2,1)S(1)} %copy-done.1), channel_id=1, source_target_pairs={{0,16},{16,0},{1,17},{17,1},{2,18},{18,2},{3,19},{19,3},{4,20},{20... | collective-permute-start | bytes 614408 | tf_op jit(solution)/shard_map/ppermute | solution.py:191
  36.5 3.1 %collective-permute-start.1 = (bf16[800,128]{1,0:T(8,128)(2,1)S(1)}, bf16[800,128]{1,0:T(8,128)(2,1)S(1)}, u32[]{:S(2)}, u32[]{:S(2)}) collective-permute-start(bf16[800,128]{1,0:T(8,128)(2,1)S(1)} %copy-done.1), channel_id=1, source_target_pairs={{0,2},{2,0},{1,3},{3,1},{4,6},{6,4},{5,7},{7,5},{8,10},{10,8},{9,1... | collective-permute-start | bytes 614408 | tf_op jit(solution)/shard_map/ppermute | solution.py:190
  39.6 0.0 collective-permute-done.3
  39.6 3.7 %collective-permute-done.2 = bf16[800,128]{1,0:T(8,128)(2,1)S(1)} collective-permute-done((bf16[800,128]{1,0:T(8,128)(2,1)S(1)}, bf16[800,128]{1,0:T(8,128)(2,1)S(1)}, u32[]{:S(2)}, u32[]{:S(2)}) %collective-permute-start.2) | collective-permute-done | bytes 204832 | tf_op jit(solution)/shard_map/ppermute | solution.py:191
  43.2 1.2 %collective-permute-done.1 = bf16[800,128]{1,0:T(8,128)(2,1)S(1)} collective-permute-done((bf16[800,128]{1,0:T(8,128)(2,1)S(1)}, bf16[800,128]{1,0:T(8,128)(2,1)S(1)}, u32[]{:S(2)}, u32[]{:S(2)}) %collective-permute-start.1) | collective-permute-done | bytes 204832 | tf_op jit(solution)/shard_map/ppermute | solution.py:190
  44.4 0.0 all-to-all-done.panels
  44.4 0.0 copy-start
  44.4 0.1 pad_maximum_fusion.near
  44.5 1.9 %collective-permute-start.4 = (bf16[4,800,128]{2,1,0:T(8,128)(2,1)S(1)}, bf16[4,800,128]{2,1,0:T(8,128)(2,1)S(1)}, u32[]{:S(2)}, u32[]{:S(2)}) collective-permute-start(bf16[4,800,128]{2,1,0:T(8,128)(2,1)S(1)} %pad_maximum_fusion.near), channel_id=1, source_target_pairs={{0,1},{1,0},{2,3},{3,2},{4,5},{5,4},{6,7},{7,6},{8,9},{9,8},{10,11... | collective-permute-start | bytes 2457608 | tf_op jit(solution)/shard_map/ppermute | solution.py:198
  46.5 2.3 %collective-permute-done.4.far = bf16[4,800,128]{2,1,0:T(8,128)(2,1)S(1)} collective-permute-done((bf16[4,800,128]{2,1,0:T(8,128)(2,1)S(1)}, bf16[4,800,128]{2,1,0:T(8,128)(2,1)S(1)}, u32[]{:S(2)}, u32[]{:S(2)}) %collective-permute-start.4) | collective-permute-done | bytes 819232 | tf_op jit(solution)/shard_map/ppermute | solution.py:198
  48.8 0.0 copy-done
  48.8 2.0 %middle.1 = f32[4,72,128]{2,1,0:T(8,128)S(1)} custom-call(bf16[4,800,128]{2,1,0:T(8,128)(2,1)S(1)} %pad_maximum_fusion.near, bf16[4,800,128]{2,1,0:T(8,128)(2,1)S(1)} %collective-permute-done.4.far, bf16[4,16,24,128]{3,2,1,0:T(8,128)(2,1)S(1)} %all-to-all-done.panels, s32[512]{0:T(512)S(1)} %copy-done), custom_call_target="tpu_custom_call" | custom-call | flops 500000000 | bytes 3000000 | tf_op jit(solution)/shard_map/middle/pallas_call | solution.py:200
  50.8 13.0 %all_to_all.15 = f32[4,72,128]{2,1,0:T(8,128)S(1)} all-to-all(f32[4,72,128]{2,1,0:T(8,128)S(1)} %middle.1), channel_id=1, replica_groups=mesh['yh'=4,'zh'=4,'zl'=2,'yl'=2,'xh'=4,'xl'=2,'k'=2] {'xh'}, dimensions={0} | all-to-all | bytes 294912 | tf_op jit(solution)/shard_map/all_to_all | solution.py:220
  63.8 12.6 %all_to_all.16.parts = f32[8,72,128]{2,1,0:T(8,128)S(1)} all-to-all(f32[8,72,128]{2,1,0:T(8,128)S(1)} %broadcast_in_dim.5), channel_id=1, replica_groups=mesh['yh'=4,'zh'=4,'zl'=2,'yl'=2,'xh'=4,'xl'=2,'k'=2] {'yl','xl','k'}, dimensions={0} | all-to-all | bytes 589824 | tf_op jit(solution)/shard_map/all_to_all | solution.py:222
  76.5 1.7 %place.1 = f32[2,24,1584]{2,1,0:T(8,128)} custom-call(f32[8,72,128]{2,1,0:T(8,128)S(1)} %all_to_all.16.parts), custom_call_target="tpu_custom_call" | custom-call | flops 1000000 | bytes 600000 | tf_op jit(solution)/shard_map/place/pallas_call | solution.py:225
  (2 shorter events, 0.0 us)
Async XLA Ops:
  0.0 8.8 %collective-permute-start = (bf16[16,24,128]{2,1,0:T(8,128)(2,1)}, bf16[16,24,128]{2,1,0:T(8,128)(2,1)S(1)}, u32[]{:S(2)}, u32[]{:S(2)}) collective-permute-start(bf16[16,24,128]{2,1,0:T(8,128)(2,1)} %refs_4_.1), channel_id=1, source_target_pairs={{0,0},{32,1},{256,2},{288,3},{4,4},{36,5},{260,6},{292,7},{8,8},{4... | collective-permute-start | bytes 294920 | tf_op jit(solution)/shard_map/ppermute | solution.py:167
  9.7 14.7 %copy-start.1 = (bf16[800,128]{1,0:T(8,128)(2,1)S(1)}, bf16[800,128]{1,0:T(8,128)(2,1)}, u32[]{:S(2)}) copy-start(bf16[800,128]{1,0:T(8,128)(2,1)} %left.1) | copy-start | bytes 614404
  9.7 34.8 %all-to-all-start = ((bf16[4,16,24,128]{3,2,1,0:T(8,128)(2,1)}), bf16[4,16,24,128]{3,2,1,0:T(8,128)(2,1)S(1)}, u32[]{:S(2)}, u32[]{:S(2)}) async-start(bf16[4,16,24,128]{3,2,1,0:T(8,128)(2,1)} %broadcast_in_dim.4), calls=%async_computation | async-start | bytes 786432 | tf_op jit(solution)/shard_map/all_to_all | solution.py:193
  24.4 15.2 %collective-permute-start.3 = (bf16[800,128]{1,0:T(8,128)(2,1)S(1)}, bf16[800,128]{1,0:T(8,128)(2,1)S(1)}, u32[]{:S(2)}, u32[]{:S(2)}) collective-permute-start(bf16[800,128]{1,0:T(8,128)(2,1)S(1)} %copy-done.1), channel_id=1, source_target_pairs={{0,18},{2,16},{16,2},{18,0},{1,19},{3,17},{17,3},{19,1},{4,22},{6,... | collective-permute-start | bytes 614408 | tf_op jit(solution)/shard_map/ppermute | solution.py:192
  33.6 9.6 %collective-permute-start.2 = (bf16[800,128]{1,0:T(8,128)(2,1)S(1)}, bf16[800,128]{1,0:T(8,128)(2,1)S(1)}, u32[]{:S(2)}, u32[]{:S(2)}) collective-permute-start(bf16[800,128]{1,0:T(8,128)(2,1)S(1)} %copy-done.1), channel_id=1, source_target_pairs={{0,16},{16,0},{1,17},{17,1},{2,18},{18,2},{3,19},{19,3},{4,20},{20... | collective-permute-start | bytes 614408 | tf_op jit(solution)/shard_map/ppermute | solution.py:191
  36.5 8.0 %collective-permute-start.1 = (bf16[800,128]{1,0:T(8,128)(2,1)S(1)}, bf16[800,128]{1,0:T(8,128)(2,1)S(1)}, u32[]{:S(2)}, u32[]{:S(2)}) collective-permute-start(bf16[800,128]{1,0:T(8,128)(2,1)S(1)} %copy-done.1), channel_id=1, source_target_pairs={{0,2},{2,0},{1,3},{3,1},{4,6},{6,4},{5,7},{7,5},{8,10},{10,8},{9,1... | collective-permute-start | bytes 614408 | tf_op jit(solution)/shard_map/ppermute | solution.py:190
  44.4 4.3 %copy-start = (s32[512]{0:T(512)S(1)}, s32[512]{0:T(512)}, u32[]{:S(2)}) copy-start(s32[512]{0:T(512)} %aggregate_far.1) | copy-start | bytes 6148
  44.5 4.2 %collective-permute-start.4 = (bf16[4,800,128]{2,1,0:T(8,128)(2,1)S(1)}, bf16[4,800,128]{2,1,0:T(8,128)(2,1)S(1)}, u32[]{:S(2)}, u32[]{:S(2)}) collective-permute-start(bf16[4,800,128]{2,1,0:T(8,128)(2,1)S(1)} %pad_maximum_fusion.near), channel_id=1, source_target_pairs={{0,1},{1,0},{2,3},{3,2},{4,5},{5,4},{6,7},{7,6},{8,9},{9,8},{10,11... | collective-permute-start | bytes 2457608 | tf_op jit(solution)/shard_map/ppermute | solution.py:198

commit v3 on v2

--- a/solution.py
+++ b/solution.py
@@ -1,3 +1,5 @@
+import functools
+
 import jax
 import jax.numpy as jnp
 import numpy as np
@@ -21,6 +23,7 @@
 AGG_DEV = 2
 PAIR = AGG_DEV * MODES
 CODES = AGG_DEV * 4 * ROWS_HERE
+EARLY = 2
 PLANES = MODES + 1
 WIN = 1584
 LIMIT = 24 * 1024 * 1024
@@ -66,13 +69,32 @@
     out[...] = wide[...].astype(jnp.bfloat16)
 
 
-def middle_kernel(near, far, panels, aggregate_far, out, wide, aggregate, arrived):
+def spread_kernel(one, out, arrived):
+    copies = [pltpu.make_async_copy(one, out.at[u], arrived.at[u]) for u in range(4)]
+    for copy in copies:
+        copy.start()
+    for copy in copies:
+        copy.wait()
+
+
+def halves_kernel(aggregate_far, out, aggregate, arrived):
     copy = pltpu.make_async_copy(aggregate_far, aggregate, arrived)
     copy.start()
+    copy.wait()
     q = lax.axis_index("yl") * 4 + lax.axis_index("xl") * 2 + lax.axis_index("k")
+    for y in range(4):
+        group = (q >> 1) * 8 + y * 2 + (q & 1)
+        for j in range(ROWS_HERE):
+            which = aggregate[group * ROWS_HERE + j] - group * AGG_DEV
+            out[pl.ds(y * ROWS_HERE + j, 1), :] = jnp.full((1, DOFS), which, jnp.int32).astype(jnp.float32)
+
+
+def middle_kernel(near, far, far_late, panels, which, out, wide):
+    q = lax.axis_index("yl") * 4 + lax.axis_index("xl") * 2 + lax.axis_index("k")
 
     def plane(m):
-        parts = [ref[u, m * SLOTS : (m + 1) * SLOTS, :] for ref in (near, far) for u in range(4)]
+        rows = slice(m * SLOTS, (m + 1) * SLOTS)
+        parts = [near[u, rows, :] for u in range(4)] + [far[u, rows, :] + far_late[u, rows, :] for u in range(4)]
         return jnp.concatenate(parts, axis=0)
 
     codes = plane(MODES).astype(jnp.float32)
@@ -82,19 +104,17 @@
         summed = jnp.dot(hot, pair, preferred_element_type=jnp.float32)
         wide[m * CODES : (m + 1) * CODES, :] = summed[:, :DOFS]
         wide[(m + 1) * CODES : (m + 2) * CODES, :] = summed[:, DOFS:]
-    copy.wait()
     found = []
     for y in range(4):
-        group = (q >> 1) * 8 + y * 2 + (q & 1)
         lefts, rights = [], []
         for j in range(ROWS_HERE):
             a0 = wide[pl.ds(y * 16 + j, MODES, stride=CODES), :]
             a1 = wide[pl.ds(64 + y * 16 + j, MODES, stride=CODES), :]
             lefts.append(jnp.concatenate([a0, a1], axis=0))
-            which = aggregate[group * ROWS_HERE + j] - group * AGG_DEV
+            side = jnp.broadcast_to(which[pl.ds(y * ROWS_HERE + j, 1), :], (MODES, DOFS))
             panel = panels[y, j].astype(jnp.float32)
             zero = jnp.zeros_like(panel)
-            halves = [jnp.where(which == b, panel, zero) for b in range(AGG_DEV)]
+            halves = [jnp.where(side == float(b), panel, zero) for b in range(AGG_DEV)]
             rights.append(jnp.concatenate(halves, axis=0).astype(jnp.bfloat16))
         left = jnp.concatenate(lefts, axis=1)
         high = left.astype(jnp.bfloat16)
@@ -184,18 +204,45 @@
         cost_estimate=pl.CostEstimate(flops=25_000_000, bytes_accessed=2_000_000, transcendentals=0),
         name="left",
     )(blocks, columns.T, counts.T, aggregate, panels)
-    left, turned = lax.optimization_barrier((left, turned))
-    swap = [(0, 1), (1, 0)]
-    cross = [(0, 3), (1, 2), (2, 1), (3, 0)]
-    beside = lax.ppermute(left, "xl", swap)
-    above = lax.ppermute(left, "yl", swap)
-    across = lax.ppermute(left, QUAD, cross)
-    gathered = lax.all_to_all(
-        jnp.broadcast_to(turned[None], (4,) + turned.shape), "zh", 0, 0, tiled=True
-    )
-    beside, above, across, gathered = lax.optimization_barrier((beside, above, across, gathered))
-    near = jnp.stack([left, beside, above, across])
-    far = lax.ppermute(near, "k", swap)
+    def flips(early, *names):
+        pairs = []
+        for at in np.ndindex(*SIZES):
+            if (at[1] < EARLY) == early:
+                to = tuple(1 - c if n in names else c for n, c in zip(AXES, at))
+                pairs.append((int(np.ravel_multi_index(at, SIZES)), int(np.ravel_multi_index(to, SIZES))))
+        return pairs
+
+    def around(x, early):
+        return [lax.ppermute(x, AXES, flips(early, *names)) for names in (("xl",), ("yl",), ("yl", "xl"))]
+
+    which = pl.pallas_call(
+        halves_kernel,
+        out_shape=jax.ShapeDtypeStruct((4 * ROWS_HERE, DOFS), f32),
+        in_specs=everything(pltpu.HBM, 1),
+        out_specs=pl.BlockSpec(memory_space=VMEM),
+        scratch_shapes=[pltpu.SMEM(aggregate.shape, jnp.int32), pltpu.SemaphoreType.DMA],
+        compiler_params=params,
+        cost_estimate=pl.CostEstimate(flops=100_000_000_000, bytes_accessed=1_000, transcendentals=0),
+        name="halves",
+    )(aggregate)
+    early = around(left, True)
+    far_early = lax.ppermute(jnp.stack([left, *early]), AXES, flips(True, "k"))
+    copies = pl.pallas_call(
+        spread_kernel,
+        out_shape=jax.ShapeDtypeStruct((4,) + turned.shape, bf16),
+        in_specs=[pl.BlockSpec(memory_space=VMEM)],
+        out_specs=pl.BlockSpec(memory_space=pl.ANY),
+        scratch_shapes=[pltpu.SemaphoreType.DMA((4,))],
+        compiler_params=params,
+        cost_estimate=pl.CostEstimate(flops=100_000_000_000, bytes_accessed=500_000, transcendentals=0),
+        name="copies",
+    )(turned)
+    gathered = lax.all_to_all(copies, "zh", 0, 0, tiled=True)
+    left_later, far_early, which = lax.optimization_barrier((left, far_early, which))
+    late = around(left_later, False)
+    late, gathered = lax.optimization_barrier((late, gathered))
+    near = jnp.stack([left, *(one + two for one, two in zip(early, late))])
+    far_late = lax.ppermute(near, AXES, flips(False, "k"))
 
     part = pl.pallas_call(
         middle_kernel,
@@ -204,18 +251,15 @@
             pl.BlockSpec(memory_space=VMEM),
             pl.BlockSpec(memory_space=VMEM),
             pl.BlockSpec(memory_space=VMEM),
-            pl.BlockSpec(memory_space=pltpu.HBM),
+            pl.BlockSpec(memory_space=VMEM),
+            pl.BlockSpec(memory_space=VMEM),
         ],
         out_specs=pl.BlockSpec(memory_space=VMEM),
-        scratch_shapes=[
-            pltpu.VMEM((MODES * CODES, DOFS), f32),
-            pltpu.SMEM(aggregate.shape, jnp.int32),
-            pltpu.SemaphoreType.DMA,
-        ],
+        scratch_shapes=[pltpu.VMEM((MODES * CODES, DOFS), f32)],
         compiler_params=params,
         cost_estimate=pl.CostEstimate(flops=500_000_000, bytes_accessed=3_000_000, transcendentals=0),
         name="middle",
-    )(near, far, gathered, aggregate)
+    )(near, far_early, far_late, gathered, which)
 
     shares = lax.all_to_all(part, "xh", 0, 0, tiled=True)
     whole = jnp.sum(shares, axis=0)

time: 78.6 us -> 74.4 us (0.947)
  starting transfers between devices: 38.1 us -> 33.1 us
  waiting for transfers between devices: 7.17 us -> 4.53 us
  blocking collectives: 25.6 us -> 28 us
  Pallas kernels: 6.22 us -> 7.42 us
  local copies, waits for them, and re-layouts: 0.84 us -> 0.03 us
    all_to_all x1, starting transfers between devices: 14.7 us -> 7.13 us  [local(): gathered = lax.all_to_all(copies, 'zh', 0, 0, tiled=True)]
    ppermute x4 -> x8, waiting for transfers between devices: 7.16 us -> 1.29 us  [the longest x1 1.27 us: local(): far_early = lax.ppermute(jnp.stack([left, *early]), AXES, flips(True, 'k'))]
    all_to_all x1, waiting for transfers between devices: 0.01 us -> 3.24 us  [local(): gathered = lax.all_to_all(copies, 'zh', 0, 0, tiled=True)]
    ppermute x4 -> x8, starting transfers between devices: 17.1 us -> 19.7 us  [the longest x6 14.9 us: around(): lax.ppermute(x, AXES, flips(early, *names))]
    all_to_all x1, blocking collectives: 13 us -> 15.3 us  [local(): shares = lax.all_to_all(part, 'xh', 0, 0, tiled=True)]
    pallas_call x0 -> x2, Pallas kernels: none -> 1.43 us  [the longest x1 0.78 us: local(): pl.pallas_call(spread_kernel, out_shape=jax.ShapeDtypeStruct((4,) + turne...]
    broadcast_in_dim x1 -> x0, local copies, waits for them, and re-layouts: 0.81 us -> none  [local(): jnp.broadcast_to(turned[None], (4,) + turned.shape)]
  transfers between devices with their start and end apart: 6 -> 10, of which waited for: 3 -> 2; matrix products, arithmetic and copies ran while one was open for 0% -> 0% of each run, Pallas kernels for 3% -> 5%
where the time goes in v3:
time: 74.4 us; the launch traced here: 73.7 us
  starting transfers between devices  33.1 us (44%)
  blocking collectives  28 us (38%)
  Pallas kernels  7.42 us (10%)
  waiting for transfers between devices  4.53 us (6%)
    all_to_all x1, blocking collectives, local(): shares = lax.all_to_all(part, 'xh', 0, 0, tiled=True)  15.3 us
    ppermute x6, starting transfers between devices, around(): lax.ppermute(x, AXES, flips(early, *names))  14.9 us
    all_to_all x1, blocking collectives, local(): lax.all_to_all(jnp.broadcast_to(whole[None], (8,) + whole.shape), SHARE,...  12.7 us
    all_to_all x1, starting transfers between devices, local(): gathered = lax.all_to_all(copies, 'zh', 0, 0, tiled=True)  7.13 us
    ppermute x1, starting transfers between devices, local(): turned = lax.ppermute(panels, AXES, pairs)  6.29 us
    ppermute x1, starting transfers between devices, local(): far_early = lax.ppermute(jnp.stack([left, *early]), AXES, flips(True, 'k'))  4.09 us
    all_to_all x1, waiting for transfers between devices, local(): gathered = lax.all_to_all(copies, 'zh', 0, 0, tiled=True)  3.24 us
    pallas_call x1, Pallas kernels, local(): pl.pallas_call(left_kernel, out_shape=jax.ShapeDtypeStruct((PLANES * SLOT...  2.53 us
  transfers between devices with their start and end apart: 10, of which 2 were waited for; matrix products, arithmetic and copies ran while one was open for 0% of the time, Pallas kernels for 5%

profile of v3, /device:TPU:1, one launch (start us, length us, event | category | flops | bytes accessed | tf_op | source)
XLA Modules:
  0.0 73.7 jit_solution(4541041212403242713)
XLA Ops:
  0.0 6.3 %collective-permute-start.7 = (bf16[16,24,128]{2,1,0:T(8,128)(2,1)}, bf16[16,24,128]{2,1,0:T(8,128)(2,1)S(1)}, u32[]{:S(2)}, u32[]{:S(2)}) collective-permute-start(bf16[16,24,128]{2,1,0:T(8,128)(2,1)} %refs_4_.1), channel_id=1, source_target_pairs={{0,0},{32,1},{256,2},{288,3},{4,4},{36,5},{260,6},{292,7},{8,8},{4... | collective-permute-start | bytes 294920 | tf_op jit(solution)/shard_map/ppermute | solution.py:187
  6.3 2.5 %left.1 = bf16[800,128]{1,0:T(8,128)(2,1)} custom-call(bf16[16,2,128,128]{3,2,1,0:T(8,128)(2,1)} %refs_0_.1, s32[2,16]{1,0:T(2,128)} %bitcast.17, s32[1,16]{1,0:T(1,128)} %bitcast.18, s32[512]{0:T(512)} %aggregate_far.1, bf16[16,24,128]{2,1,0:T(8,128)(2,1)} %refs_4_.1), custom_call_target="tpu_custom_call" | custom-call | flops 25000000 | bytes 2000000 | tf_op jit(solution)/shard_map/left/pallas_call | solution.py:189
  8.8 8.4 %collective-permute-start.2 = (bf16[800,128]{1,0:T(8,128)(2,1)}, bf16[800,128]{1,0:T(8,128)(2,1)S(1)}, u32[]{:S(2)}, u32[]{:S(2)}) collective-permute-start(bf16[800,128]{1,0:T(8,128)(2,1)} %left.1), channel_id=1, source_target_pairs={{0,18},{1,19},{2,16},{3,17},{4,22},{5,23},{6,20},{7,21},{8,26},{9,... | collective-permute-start | bytes 614408 | tf_op jit(solution)/shard_map/ppermute | solution.py:216
  17.2 1.9 %collective-permute-start.1 = (bf16[800,128]{1,0:T(8,128)(2,1)}, bf16[800,128]{1,0:T(8,128)(2,1)S(1)}, u32[]{:S(2)}, u32[]{:S(2)}) collective-permute-start(bf16[800,128]{1,0:T(8,128)(2,1)} %left.1), channel_id=1, source_target_pairs={{0,16},{1,17},{2,18},{3,19},{4,20},{5,21},{6,22},{7,23},{8,24},{9,... | collective-permute-start | bytes 614408 | tf_op jit(solution)/shard_map/ppermute | solution.py:216
  19.1 2.6 %collective-permute-start = (bf16[800,128]{1,0:T(8,128)(2,1)}, bf16[800,128]{1,0:T(8,128)(2,1)S(1)}, u32[]{:S(2)}, u32[]{:S(2)}) collective-permute-start(bf16[800,128]{1,0:T(8,128)(2,1)} %left.1), channel_id=1, source_target_pairs={{0,2},{1,3},{2,0},{3,1},{4,6},{5,7},{6,4},{7,5},{8,10},{9,11},{10,... | collective-permute-start | bytes 614408 | tf_op jit(solution)/shard_map/ppermute | solution.py:216
  21.8 0.0 collective-permute-done.7.one
  21.8 0.8 %copies.1 = bf16[4,16,24,128]{3,2,1,0:T(8,128)(2,1)} custom-call(bf16[16,24,128]{2,1,0:T(8,128)(2,1)S(1)} %collective-permute-done.7.one), custom_call_target="tpu_custom_call" | custom-call | flops 99999997952 | bytes 500000 | tf_op jit(solution)/shard_map/copies/pallas_call | solution.py:230
  22.6 0.0 copy-start.1
  22.6 7.1 %all-to-all-start = ((bf16[4,16,24,128]{3,2,1,0:T(8,128)(2,1)}), bf16[4,16,24,128]{3,2,1,0:T(8,128)(2,1)S(1)}, u32[]{:S(2)}, u32[]{:S(2)}) async-start(bf16[4,16,24,128]{3,2,1,0:T(8,128)(2,1)} %copies.1), calls=%async_computation | async-start | bytes 786432 | tf_op jit(solution)/shard_map/all_to_all | solution.py:240
  29.7 0.0 collective-permute-done.2
  29.7 0.0 collective-permute-done.1
  29.7 0.0 collective-permute-done
  29.7 0.0 copy-done.1
  29.8 0.0 copy-start
  29.8 0.1 fusion.3
  29.9 4.1 %collective-permute-start.3 = (bf16[4,800,128]{2,1,0:T(8,128)(2,1)S(1)}, bf16[4,800,128]{2,1,0:T(8,128)(2,1)S(1)}, u32[]{:S(2)}, u32[]{:S(2)}) collective-permute-start(bf16[4,800,128]{2,1,0:T(8,128)(2,1)S(1)} %fusion.3), channel_id=1, source_target_pairs={{0,1},{1,0},{2,3},{3,2},{4,5},{5,4},{6,7},{7,6},{8,9},{9,8},{10,11... | collective-permute-start | bytes 2457608 | tf_op jit(solution)/shard_map/ppermute | solution.py:229
  34.0 0.0 copy-done
  34.0 0.6 halves.1.which
  34.6 1.3 %collective-permute-done.3.far = bf16[4,800,128]{2,1,0:T(8,128)(2,1)S(1)} collective-permute-done((bf16[4,800,128]{2,1,0:T(8,128)(2,1)S(1)}, bf16[4,800,128]{2,1,0:T(8,128)(2,1)S(1)}, u32[]{:S(2)}, u32[]{:S(2)}) %collective-permute-start.3) | collective-permute-done | bytes 819232 | tf_op jit(solution)/shard_map/ppermute | solution.py:229
  35.9 0.7 collective-permute-start.6
  36.6 0.7 collective-permute-start.5
  37.3 0.7 collective-permute-start.4
  37.9 3.2 %all-to-all-done.panels = bf16[4,16,24,128]{3,2,1,0:T(8,128)(2,1)S(1)} async-done(((bf16[4,16,24,128]{3,2,1,0:T(8,128)(2,1)}), bf16[4,16,24,128]{3,2,1,0:T(8,128)(2,1)S(1)}, u32[]{:S(2)}, u32[]{:S(2)}) %all-to-all-start) | async-done | bytes 393248 | tf_op jit(solution)/shard_map/all_to_all | solution.py:240
  41.2 0.0 collective-permute-done.6
  41.2 0.0 collective-permute-done.5
  41.2 0.0 collective-permute-done.4
  41.2 0.1 add_bitcast_fusion
  41.3 0.1 fusion.1.near
  41.4 0.7 collective-permute-start.8
  42.1 0.0 collective-permute-done.8.far_late
  42.1 1.8 %middle.1 = f32[4,72,128]{2,1,0:T(8,128)S(1)} custom-call(bf16[4,800,128]{2,1,0:T(8,128)(2,1)S(1)} %fusion.1.near, bf16[4,800,128]{2,1,0:T(8,128)(2,1)S(1)} %collective-permute-done.3.far, bf16[4,800,128]{2,1,0:T(8,128)(2,1)S(1)} %collective-permute-done.8.far_late, bf16[4,16,24,128]{3,2,1,0:T(8,128)(2,1)S(1)} %all-to-all-done.panels, f32[64,128]{1,0:T(8,128)S(1)} %halves.1.which), custom_call_target="tpu_custom_call" | custom-call | flops 500000000 | bytes 3000000 | tf_op jit(solution)/shard_map/middle/pallas_call | solution.py:247
  43.9 15.3 %all_to_all.15 = f32[4,72,128]{2,1,0:T(8,128)S(1)} all-to-all(f32[4,72,128]{2,1,0:T(8,128)S(1)} %middle.1), channel_id=1, replica_groups=mesh['yh'=4,'zh'=4,'zl'=2,'yl'=2,'xh'=4,'xl'=2,'k'=2] {'xh'}, dimensions={0} | all-to-all | bytes 294912 | tf_op jit(solution)/shard_map/all_to_all | solution.py:264
  59.3 12.7 %all_to_all.16.parts = f32[8,72,128]{2,1,0:T(8,128)S(1)} all-to-all(f32[8,72,128]{2,1,0:T(8,128)S(1)} %broadcast_in_dim.2), channel_id=1, replica_groups=mesh['yh'=4,'zh'=4,'zl'=2,'yl'=2,'xh'=4,'xl'=2,'k'=2] {'yl','xl','k'}, dimensions={0} | all-to-all | bytes 589824 | tf_op jit(solution)/shard_map/all_to_all | solution.py:266
  72.0 1.7 %place.1 = f32[2,24,1584]{2,1,0:T(8,128)} custom-call(f32[8,72,128]{2,1,0:T(8,128)S(1)} %all_to_all.16.parts), custom_call_target="tpu_custom_call" | custom-call | flops 1000000 | bytes 600000 | tf_op jit(solution)/shard_map/place/pallas_call | solution.py:269
  (3 shorter events, 0.1 us)
Async XLA Ops:
  0.0 21.8 %collective-permute-start.7 = (bf16[16,24,128]{2,1,0:T(8,128)(2,1)}, bf16[16,24,128]{2,1,0:T(8,128)(2,1)S(1)}, u32[]{:S(2)}, u32[]{:S(2)}) collective-permute-start(bf16[16,24,128]{2,1,0:T(8,128)(2,1)} %refs_4_.1), channel_id=1, source_target_pairs={{0,0},{32,1},{256,2},{288,3},{4,4},{36,5},{260,6},{292,7},{8,8},{4... | collective-permute-start | bytes 294920 | tf_op jit(solution)/shard_map/ppermute | solution.py:187
  8.8 20.9 %collective-permute-start.2 = (bf16[800,128]{1,0:T(8,128)(2,1)}, bf16[800,128]{1,0:T(8,128)(2,1)S(1)}, u32[]{:S(2)}, u32[]{:S(2)}) collective-permute-start(bf16[800,128]{1,0:T(8,128)(2,1)} %left.1), channel_id=1, source_target_pairs={{0,18},{1,19},{2,16},{3,17},{4,22},{5,23},{6,20},{7,21},{8,26},{9,... | collective-permute-start | bytes 614408 | tf_op jit(solution)/shard_map/ppermute | solution.py:216
  17.2 12.5 %collective-permute-start.1 = (bf16[800,128]{1,0:T(8,128)(2,1)}, bf16[800,128]{1,0:T(8,128)(2,1)S(1)}, u32[]{:S(2)}, u32[]{:S(2)}) collective-permute-start(bf16[800,128]{1,0:T(8,128)(2,1)} %left.1), channel_id=1, source_target_pairs={{0,16},{1,17},{2,18},{3,19},{4,20},{5,21},{6,22},{7,23},{8,24},{9,... | collective-permute-start | bytes 614408 | tf_op jit(solution)/shard_map/ppermute | solution.py:216
  19.1 10.6 %collective-permute-start = (bf16[800,128]{1,0:T(8,128)(2,1)}, bf16[800,128]{1,0:T(8,128)(2,1)S(1)}, u32[]{:S(2)}, u32[]{:S(2)}) collective-permute-start(bf16[800,128]{1,0:T(8,128)(2,1)} %left.1), channel_id=1, source_target_pairs={{0,2},{1,3},{2,0},{3,1},{4,6},{5,7},{6,4},{7,5},{8,10},{9,11},{10,... | collective-permute-start | bytes 614408 | tf_op jit(solution)/shard_map/ppermute | solution.py:216
  22.6 7.2 %copy-start.1 = (bf16[800,128]{1,0:T(8,128)(2,1)S(1)}, bf16[800,128]{1,0:T(8,128)(2,1)}, u32[]{:S(2)}) copy-start(bf16[800,128]{1,0:T(8,128)(2,1)} %left.1) | copy-start | bytes 614404
  22.6 18.6 %all-to-all-start = ((bf16[4,16,24,128]{3,2,1,0:T(8,128)(2,1)}), bf16[4,16,24,128]{3,2,1,0:T(8,128)(2,1)S(1)}, u32[]{:S(2)}, u32[]{:S(2)}) async-start(bf16[4,16,24,128]{3,2,1,0:T(8,128)(2,1)} %copies.1), calls=%async_computation | async-start | bytes 786432 | tf_op jit(solution)/shard_map/all_to_all | solution.py:240
  29.8 4.2 %copy-start = (s32[512]{0:T(512)S(1)}, s32[512]{0:T(512)}, u32[]{:S(2)}) copy-start(s32[512]{0:T(512)} %aggregate_far.1) | copy-start | bytes 6148
  29.9 6.0 %collective-permute-start.3 = (bf16[4,800,128]{2,1,0:T(8,128)(2,1)S(1)}, bf16[4,800,128]{2,1,0:T(8,128)(2,1)S(1)}, u32[]{:S(2)}, u32[]{:S(2)}) collective-permute-start(bf16[4,800,128]{2,1,0:T(8,128)(2,1)S(1)} %fusion.3), channel_id=1, source_target_pairs={{0,1},{1,0},{2,3},{3,2},{4,5},{5,4},{6,7},{7,6},{8,9},{9,8},{10,11... | collective-permute-start | bytes 2457608 | tf_op jit(solution)/shard_map/ppermute | solution.py:229
  35.9 5.3 %collective-permute-start.6 = (bf16[800,128]{1,0:T(8,128)(2,1)S(1)}, bf16[800,128]{1,0:T(8,128)(2,1)S(1)}, u32[]{:S(2)}, u32[]{:S(2)}) collective-permute-start(bf16[800,128]{1,0:T(8,128)(2,1)S(1)} %copy-done.1), channel_id=1, source_target_pairs={{128,146},{129,147},{130,144},{131,145},{132,150},{133,151},{134,1... | collective-permute-start | bytes 614408 | tf_op jit(solution)/shard_map/ppermute | solution.py:216
  36.6 4.6 %collective-permute-start.5 = (bf16[800,128]{1,0:T(8,128)(2,1)S(1)}, bf16[800,128]{1,0:T(8,128)(2,1)S(1)}, u32[]{:S(2)}, u32[]{:S(2)}) collective-permute-start(bf16[800,128]{1,0:T(8,128)(2,1)S(1)} %copy-done.1), channel_id=1, source_target_pairs={{128,144},{129,145},{130,146},{131,147},{132,148},{133,149},{134,1... | collective-permute-start | bytes 614408 | tf_op jit(solution)/shard_map/ppermute | solution.py:216
  37.3 3.9 %collective-permute-start.4 = (bf16[800,128]{1,0:T(8,128)(2,1)S(1)}, bf16[800,128]{1,0:T(8,128)(2,1)S(1)}, u32[]{:S(2)}, u32[]{:S(2)}) collective-permute-start(bf16[800,128]{1,0:T(8,128)(2,1)S(1)} %copy-done.1), channel_id=1, source_target_pairs={{128,130},{129,131},{130,128},{131,129},{132,134},{133,135},{134,1... | collective-permute-start | bytes 614408 | tf_op jit(solution)/shard_map/ppermute | solution.py:216
  41.4 0.7 collective-permute-start.8

commit v4 on v3

--- a/solution.py
+++ b/solution.py
@@ -28,6 +28,15 @@
 WIN = 1584
 LIMIT = 24 * 1024 * 1024
 FULL = 63 * 1024 * 1024
+
+
+def member(yh, ahead):
+    odd = ahead & 1
+    return odd * (4 - ahead) + (1 - odd) * 2 * ((ahead >> 1) ^ (yh >> 1))
+
+
+def ahead_of(yh, yl, xl):
+    return xl * (3 - 2 * yl) + (1 - xl) * 2 * (yl ^ (yh >> 1))
 
 
 def left_kernel(*refs):
@@ -47,6 +56,7 @@
     for copy in copies[:3]:
         copy.wait()
     row = lax.axis_index("yh") * 8 + lax.axis_index("zh") * 2 + lax.axis_index("zl")
+    yh, zl = lax.axis_index("yh"), lax.axis_index("zl")
     lane = lax.broadcasted_iota(jnp.int32, (1, DOFS), 1)
     for i in range(ROWS_HERE):
         count = counts[0, i]
@@ -55,9 +65,9 @@
             column = columns[s, i]
             code = own * 64 + ((column >> 5) & 3) * 16 + (column & 15)
             code = jnp.where(s < count, code, -1)
-            place = ((column >> 7) * 2 + ((column >> 4) & 1)).astype(jnp.float32)
+            place = member(yh, ((column >> 7) - yh) & 3) * 2 + (((column >> 4) & 1) ^ zl)
             at = MODES * SLOTS + 2 * i + s
-            wide[pl.ds(at, 1), :] = jnp.where(lane == code, place, -1.0)
+            wide[pl.ds(at, 1), :] = jnp.where(lane == code, place, -1).astype(jnp.float32)
     copies[3].wait()
     for i in range(ROWS_HERE):
         if i % step == 0:
@@ -81,9 +91,11 @@
     copy = pltpu.make_async_copy(aggregate_far, aggregate, arrived)
     copy.start()
     copy.wait()
-    q = lax.axis_index("yl") * 4 + lax.axis_index("xl") * 2 + lax.axis_index("k")
+    yh = lax.axis_index("yh")
+    high = (yh + ahead_of(yh, lax.axis_index("yl"), lax.axis_index("xl"))) & 3
+    low = lax.axis_index("zl") ^ lax.axis_index("k")
     for y in range(4):
-        group = (q >> 1) * 8 + y * 2 + (q & 1)
+        group = high * 8 + y * 2 + low
         for j in range(ROWS_HERE):
             which = aggregate[group * ROWS_HERE + j] - group * AGG_DEV
             out[pl.ds(y * ROWS_HERE + j, 1), :] = jnp.full((1, DOFS), which, jnp.int32).astype(jnp.float32)
@@ -134,25 +146,24 @@
 
 
 def place_kernel(parts, out, wide):
-    row = lax.axis_index("yh") * 8 + lax.axis_index("zh") * 2 + lax.axis_index("zl")
-    lane = lax.broadcasted_iota(jnp.int32, (PAIR, 256), 1)
-    windows = [jnp.zeros((PAIR, 256), jnp.float32) for _ in range(6)]
-    for q in range(8):
-        rest = parts[q, PAIR:, :]
-        tail = jnp.concatenate([rest, pltpu.roll(rest, 64, axis=1)], axis=0)
-        source = jnp.concatenate([parts[q, :PAIR, :], tail], axis=1)
-        for y in range(4):
-            start = ((q >> 1) * 8 + y * 2 + (q & 1)) * PAIR
-            at = start % 256
-            turned = pltpu.roll(source, (start - y * PAIR) % 256, axis=1)
-            w = start // 256
-            windows[w] = jnp.where((lane >= at) & (lane < at + PAIR), turned, windows[w])
-            if at + PAIR > 256:
-                windows[w + 1] = jnp.where(lane < at + PAIR - 256, turned, windows[w + 1])
+    yh, zl = lax.axis_index("yh"), lax.axis_index("zl")
+    row = yh * 8 + lax.axis_index("zh") * 2 + zl
+    lane = lax.broadcasted_iota(jnp.int32, (PAIR, 384), 1)
     wide[:, : 6 * 128] = jnp.zeros((PAIR, 6 * 128), jnp.float32)
     wide[:, 18 * 128 :] = jnp.zeros((PAIR, 7 * 128), jnp.float32)
-    for w in range(6):
-        wide[:, (6 + 2 * w) * 128 : (8 + 2 * w) * 128] = windows[w]
+    for ahead in range(4):
+        block = jnp.zeros((PAIR, 384), jnp.float32)
+        for low in range(2):
+            part = parts[member(yh, ahead) * 2 + (low ^ zl)]
+            rest = part[PAIR:, :]
+            tail = jnp.concatenate([rest, pltpu.roll(rest, 64, axis=1)], axis=0)
+            source = jnp.concatenate([part[:PAIR, :], tail, jnp.zeros_like(tail)], axis=1)
+            for y in range(4):
+                start = (y * 2 + low) * PAIR
+                turned = pltpu.roll(source, (start - y * PAIR) % 384, axis=1)
+                block = jnp.where((lane >= start) & (lane < start + PAIR), turned, block)
+        at = (6 + 3 * ((yh + ahead) & 3)) * 128
+        wide[:, pl.ds(pl.multiple_of(at, 128), 384)] = block
     offset = row * PAIR
     base = pl.multiple_of((offset // 128) * 128, 128)
     shift = offset % 128
@@ -181,7 +192,9 @@
 
     pairs = []
     for yh, zh, zl, yl, xh, xl, k in np.ndindex(*SIZES):
-        source = (yl * 2 + xl, zh, k, yh >> 1, xh, yh & 1, zl)
+        ahead = ahead_of(yh, yl, xl)
+        other = 1 - yl if ahead else yl
+        source = ((yh + ahead) & 3, zh, zl ^ k, other, xh, xl, k)
         target = (yh, zh, zl, yl, xh, xl, k)
         pairs.append(tuple(int(np.ravel_multi_index(at, SIZES)) for at in (source, target)))
     turned = lax.ppermute(panels, AXES, pairs)
@@ -204,16 +217,19 @@
         cost_estimate=pl.CostEstimate(flops=25_000_000, bytes_accessed=2_000_000, transcendentals=0),
         name="left",
     )(blocks, columns.T, counts.T, aggregate, panels)
-    def flips(early, *names):
+    def flips(groups, *names):
         pairs = []
         for at in np.ndindex(*SIZES):
-            if (at[1] < EARLY) == early:
+            if at[1] in groups:
                 to = tuple(1 - c if n in names else c for n, c in zip(AXES, at))
                 pairs.append((int(np.ravel_multi_index(at, SIZES)), int(np.ravel_multi_index(to, SIZES))))
         return pairs
 
-    def around(x, early):
-        return [lax.ppermute(x, AXES, flips(early, *names)) for names in (("xl",), ("yl",), ("yl", "xl"))]
+    def swapped(x, groups, *names):
+        return lax.ppermute(x, AXES, flips(groups, *names))
+
+    first, last = range(EARLY), range(EARLY, SIZES[1])
+    most, least = range(EARLY + 1), range(EARLY + 1, SIZES[1])
 
     which = pl.pallas_call(
         halves_kernel,
@@ -225,8 +241,9 @@
         cost_estimate=pl.CostEstimate(flops=100_000_000_000, bytes_accessed=1_000, transcendentals=0),
         name="halves",
     )(aggregate)
-    early = around(left, True)
-    far_early = lax.ppermute(jnp.stack([left, *early]), AXES, flips(True, "k"))
+    across = swapped(left, most, "yl", "xl")
+    early = [swapped(left, first, "xl"), swapped(left, first, "yl")]
+    far_early = swapped(jnp.stack([left, *early, across]), first, "k")
     copies = pl.pallas_call(
         spread_kernel,
         out_shape=jax.ShapeDtypeStruct((4,) + turned.shape, bf16),
@@ -239,10 +256,11 @@
     )(turned)
     gathered = lax.all_to_all(copies, "zh", 0, 0, tiled=True)
     left_later, far_early, which = lax.optimization_barrier((left, far_early, which))
-    late = around(left_later, False)
+    late = [swapped(left_later, last, "xl"), swapped(left_later, last, "yl")]
+    late.append(swapped(left_later, least, "yl", "xl"))
     late, gathered = lax.optimization_barrier((late, gathered))
-    near = jnp.stack([left, *(one + two for one, two in zip(early, late))])
-    far_late = lax.ppermute(near, AXES, flips(False, "k"))
+    near = jnp.stack([left, *(one + two for one, two in zip([*early, across], late))])
+    far_late = swapped(near, last, "k")
 
     part = pl.pallas_call(
         middle_kernel,

time: 74.4 us -> 73.4 us (0.987)
  waiting for transfers between devices: 4.53 us -> 2.04 us
  blocking collectives: 28 us -> 29.8 us
    all_to_all x1, waiting for transfers between devices: 3.24 us -> 0.76 us  [local(): gathered = lax.all_to_all(copies, 'zh', 0, 0, tiled=True)]
    all_to_all x1, blocking collectives: 12.7 us -> 15 us  [local(): lax.all_to_all(jnp.broadcast_to(whole[None], (8,) + whole.shape), SHARE,...]
where the time goes in v4:
time: 73.4 us; the launch traced here: 72.9 us
  starting transfers between devices  33.1 us (45%)
  blocking collectives  29.8 us (41%)
  Pallas kernels  7.38 us (10%)
  waiting for transfers between devices  2.04 us (3%)
    ppermute x8, starting transfers between devices, swapped(): return lax.ppermute(x, AXES, flips(groups, *names))  20.3 us
    all_to_all x1, blocking collectives, local(): lax.all_to_all(jnp.broadcast_to(whole[None], (8,) + whole.shape), SHARE,...  15 us
    all_to_all x1, blocking collectives, local(): shares = lax.all_to_all(part, 'xh', 0, 0, tiled=True)  14.8 us
    all_to_all x1, starting transfers between devices, local(): gathered = lax.all_to_all(copies, 'zh', 0, 0, tiled=True)  7.13 us
    ppermute x1, starting transfers between devices, local(): turned = lax.ppermute(panels, AXES, pairs)  5.73 us
    pallas_call x1, Pallas kernels, local(): pl.pallas_call(left_kernel, out_shape=jax.ShapeDtypeStruct((PLANES * SLOT...  2.53 us
    pallas_call x1, Pallas kernels, local(): pl.pallas_call(middle_kernel, out_shape=jax.ShapeDtypeStruct((4, PAIR + M...  1.77 us
    pallas_call x1, Pallas kernels, local(): pl.pallas_call(place_kernel, out_shape=jax.ShapeDtypeStruct((AGG_DEV, MOD...  1.64 us
  transfers between devices with their start and end apart: 10, of which 2 were waited for; matrix products, arithmetic and copies ran while one was open for 0% of the time, Pallas kernels for 5%

profile of v4, /device:TPU:1, one launch (start us, length us, event | category | flops | bytes accessed | tf_op | source)
XLA Modules:
  0.0 72.9 jit_solution(12193100400868293966)
XLA Ops:
  0.0 5.7 %collective-permute-start.7 = (bf16[16,24,128]{2,1,0:T(8,128)(2,1)}, bf16[16,24,128]{2,1,0:T(8,128)(2,1)S(1)}, u32[]{:S(2)}, u32[]{:S(2)}) collective-permute-start(bf16[16,24,128]{2,1,0:T(8,128)(2,1)} %refs_4_.1), channel_id=1, source_target_pairs={{0,0},{33,1},{786,2},{819,3},{4,4},{37,5},{790,6},{823,7},{8,8},{4... | collective-permute-start | bytes 294920 | tf_op jit(solution)/shard_map/ppermute | solution.py:200
  5.7 2.5 %left.1 = bf16[800,128]{1,0:T(8,128)(2,1)} custom-call(bf16[16,2,128,128]{3,2,1,0:T(8,128)(2,1)} %refs_0_.1, s32[2,16]{1,0:T(2,128)} %bitcast.17, s32[1,16]{1,0:T(1,128)} %bitcast.18, s32[512]{0:T(512)} %aggregate_far.1, bf16[16,24,128]{2,1,0:T(8,128)(2,1)} %refs_4_.1), custom_call_target="tpu_custom_call" | custom-call | flops 25000000 | bytes 2000000 | tf_op jit(solution)/shard_map/left/pallas_call | solution.py:202
  8.3 5.4 %collective-permute-start.2 = (bf16[800,128]{1,0:T(8,128)(2,1)}, bf16[800,128]{1,0:T(8,128)(2,1)S(1)}, u32[]{:S(2)}, u32[]{:S(2)}) collective-permute-start(bf16[800,128]{1,0:T(8,128)(2,1)} %left.1), channel_id=1, source_target_pairs={{0,18},{1,19},{2,16},{3,17},{4,22},{5,23},{6,20},{7,21},{8,26},{9,... | collective-permute-start | bytes 614408 | tf_op jit(solution)/shard_map/ppermute | solution.py:229
  13.7 4.5 %collective-permute-start.1 = (bf16[800,128]{1,0:T(8,128)(2,1)}, bf16[800,128]{1,0:T(8,128)(2,1)S(1)}, u32[]{:S(2)}, u32[]{:S(2)}) collective-permute-start(bf16[800,128]{1,0:T(8,128)(2,1)} %left.1), channel_id=1, source_target_pairs={{0,16},{1,17},{2,18},{3,19},{4,20},{5,21},{6,22},{7,23},{8,24},{9,... | collective-permute-start | bytes 614408 | tf_op jit(solution)/shard_map/ppermute | solution.py:229
  18.2 3.0 %collective-permute-start = (bf16[800,128]{1,0:T(8,128)(2,1)}, bf16[800,128]{1,0:T(8,128)(2,1)S(1)}, u32[]{:S(2)}, u32[]{:S(2)}) collective-permute-start(bf16[800,128]{1,0:T(8,128)(2,1)} %left.1), channel_id=1, source_target_pairs={{0,2},{1,3},{2,0},{3,1},{4,6},{5,7},{6,4},{7,5},{8,10},{9,11},{10,... | collective-permute-start | bytes 614408 | tf_op jit(solution)/shard_map/ppermute | solution.py:229
  21.2 0.0 collective-permute-done.7.one
  21.2 0.8 %copies.1 = bf16[4,16,24,128]{3,2,1,0:T(8,128)(2,1)} custom-call(bf16[16,24,128]{2,1,0:T(8,128)(2,1)S(1)} %collective-permute-done.7.one), custom_call_target="tpu_custom_call" | custom-call | flops 99999997952 | bytes 500000 | tf_op jit(solution)/shard_map/copies/pallas_call | solution.py:247
  22.0 0.0 copy-start.1
  22.0 7.1 %all-to-all-start = ((bf16[4,16,24,128]{3,2,1,0:T(8,128)(2,1)}), bf16[4,16,24,128]{3,2,1,0:T(8,128)(2,1)S(1)}, u32[]{:S(2)}, u32[]{:S(2)}) async-start(bf16[4,16,24,128]{3,2,1,0:T(8,128)(2,1)} %copies.1), calls=%async_computation | async-start | bytes 786432 | tf_op jit(solution)/shard_map/all_to_all | solution.py:257
  29.2 0.0 collective-permute-done.2
  29.2 0.0 collective-permute-done.1
  29.2 0.0 collective-permute-done
  29.2 0.0 copy-done.1
  29.2 0.0 copy-start
  29.2 0.1 fusion.3
  29.3 4.6 %collective-permute-start.3 = (bf16[4,800,128]{2,1,0:T(8,128)(2,1)S(1)}, bf16[4,800,128]{2,1,0:T(8,128)(2,1)S(1)}, u32[]{:S(2)}, u32[]{:S(2)}) collective-permute-start(bf16[4,800,128]{2,1,0:T(8,128)(2,1)S(1)} %fusion.3), channel_id=1, source_target_pairs={{0,1},{1,0},{2,3},{3,2},{4,5},{5,4},{6,7},{7,6},{8,9},{9,8},{10,11... | collective-permute-start | bytes 2457608 | tf_op jit(solution)/shard_map/ppermute | solution.py:229
  34.0 0.0 copy-done
  34.0 0.7 halves.1.which
  34.6 1.3 %collective-permute-done.3.far = bf16[4,800,128]{2,1,0:T(8,128)(2,1)S(1)} collective-permute-done((bf16[4,800,128]{2,1,0:T(8,128)(2,1)S(1)}, bf16[4,800,128]{2,1,0:T(8,128)(2,1)S(1)}, u32[]{:S(2)}, u32[]{:S(2)}) %collective-permute-start.3) | collective-permute-done | bytes 819232 | tf_op jit(solution)/shard_map/ppermute | solution.py:229
  35.9 0.7 collective-permute-start.6
  36.6 0.7 collective-permute-start.5
  37.3 0.7 collective-permute-start.4
  37.9 0.8 %all-to-all-done.panels = bf16[4,16,24,128]{3,2,1,0:T(8,128)(2,1)S(1)} async-done(((bf16[4,16,24,128]{3,2,1,0:T(8,128)(2,1)}), bf16[4,16,24,128]{3,2,1,0:T(8,128)(2,1)S(1)}, u32[]{:S(2)}, u32[]{:S(2)}) %all-to-all-start) | async-done | bytes 393248 | tf_op jit(solution)/shard_map/all_to_all | solution.py:257
  38.7 0.0 collective-permute-done.6
  38.7 0.0 collective-permute-done.5
  38.7 0.0 collective-permute-done.4
  38.7 0.1 add_bitcast_fusion
  38.8 0.1 fusion.1.near
  38.9 0.7 collective-permute-start.8
  39.6 0.0 collective-permute-done.8.far_late
  39.6 1.8 %middle.1 = f32[4,72,128]{2,1,0:T(8,128)S(1)} custom-call(bf16[4,800,128]{2,1,0:T(8,128)(2,1)S(1)} %fusion.1.near, bf16[4,800,128]{2,1,0:T(8,128)(2,1)S(1)} %collective-permute-done.3.far, bf16[4,800,128]{2,1,0:T(8,128)(2,1)S(1)} %collective-permute-done.8.far_late, bf16[4,16,24,128]{3,2,1,0:T(8,128)(2,1)S(1)} %all-to-all-done.panels, f32[64,128]{1,0:T(8,128)S(1)} %halves.1.which), custom_call_target="tpu_custom_call" | custom-call | flops 500000000 | bytes 3000000 | tf_op jit(solution)/shard_map/middle/pallas_call | solution.py:265
  41.4 14.8 %all_to_all.15 = f32[4,72,128]{2,1,0:T(8,128)S(1)} all-to-all(f32[4,72,128]{2,1,0:T(8,128)S(1)} %middle.1), channel_id=1, replica_groups=mesh['yh'=4,'zh'=4,'zl'=2,'yl'=2,'xh'=4,'xl'=2,'k'=2] {'xh'}, dimensions={0} | all-to-all | bytes 294912 | tf_op jit(solution)/shard_map/all_to_all | solution.py:282
  56.3 15.0 %all_to_all.16.parts = f32[8,72,128]{2,1,0:T(8,128)S(1)} all-to-all(f32[8,72,128]{2,1,0:T(8,128)S(1)} %broadcast_in_dim.2), channel_id=1, replica_groups=mesh['yh'=4,'zh'=4,'zl'=2,'yl'=2,'xh'=4,'xl'=2,'k'=2] {'yl','xl','k'}, dimensions={0} | all-to-all | bytes 589824 | tf_op jit(solution)/shard_map/all_to_all | solution.py:284
  71.3 1.6 %place.1 = f32[2,24,1584]{2,1,0:T(8,128)} custom-call(f32[8,72,128]{2,1,0:T(8,128)S(1)} %all_to_all.16.parts), custom_call_target="tpu_custom_call" | custom-call | flops 1000000 | bytes 600000 | tf_op jit(solution)/shard_map/place/pallas_call | solution.py:287
  (3 shorter events, 0.1 us)
Async XLA Ops:
  0.0 21.2 %collective-permute-start.7 = (bf16[16,24,128]{2,1,0:T(8,128)(2,1)}, bf16[16,24,128]{2,1,0:T(8,128)(2,1)S(1)}, u32[]{:S(2)}, u32[]{:S(2)}) collective-permute-start(bf16[16,24,128]{2,1,0:T(8,128)(2,1)} %refs_4_.1), channel_id=1, source_target_pairs={{0,0},{33,1},{786,2},{819,3},{4,4},{37,5},{790,6},{823,7},{8,8},{4... | collective-permute-start | bytes 294920 | tf_op jit(solution)/shard_map/ppermute | solution.py:200
  8.3 20.9 %collective-permute-start.2 = (bf16[800,128]{1,0:T(8,128)(2,1)}, bf16[800,128]{1,0:T(8,128)(2,1)S(1)}, u32[]{:S(2)}, u32[]{:S(2)}) collective-permute-start(bf16[800,128]{1,0:T(8,128)(2,1)} %left.1), channel_id=1, source_target_pairs={{0,18},{1,19},{2,16},{3,17},{4,22},{5,23},{6,20},{7,21},{8,26},{9,... | collective-permute-start | bytes 614408 | tf_op jit(solution)/shard_map/ppermute | solution.py:229
  13.7 15.5 %collective-permute-start.1 = (bf16[800,128]{1,0:T(8,128)(2,1)}, bf16[800,128]{1,0:T(8,128)(2,1)S(1)}, u32[]{:S(2)}, u32[]{:S(2)}) collective-permute-start(bf16[800,128]{1,0:T(8,128)(2,1)} %left.1), channel_id=1, source_target_pairs={{0,16},{1,17},{2,18},{3,19},{4,20},{5,21},{6,22},{7,23},{8,24},{9,... | collective-permute-start | bytes 614408 | tf_op jit(solution)/shard_map/ppermute | solution.py:229
  18.2 11.0 %collective-permute-start = (bf16[800,128]{1,0:T(8,128)(2,1)}, bf16[800,128]{1,0:T(8,128)(2,1)S(1)}, u32[]{:S(2)}, u32[]{:S(2)}) collective-permute-start(bf16[800,128]{1,0:T(8,128)(2,1)} %left.1), channel_id=1, source_target_pairs={{0,2},{1,3},{2,0},{3,1},{4,6},{5,7},{6,4},{7,5},{8,10},{9,11},{10,... | collective-permute-start | bytes 614408 | tf_op jit(solution)/shard_map/ppermute | solution.py:229
  22.0 7.2 %copy-start.1 = (bf16[800,128]{1,0:T(8,128)(2,1)S(1)}, bf16[800,128]{1,0:T(8,128)(2,1)}, u32[]{:S(2)}) copy-start(bf16[800,128]{1,0:T(8,128)(2,1)} %left.1) | copy-start | bytes 614404
  22.0 16.7 %all-to-all-start = ((bf16[4,16,24,128]{3,2,1,0:T(8,128)(2,1)}), bf16[4,16,24,128]{3,2,1,0:T(8,128)(2,1)S(1)}, u32[]{:S(2)}, u32[]{:S(2)}) async-start(bf16[4,16,24,128]{3,2,1,0:T(8,128)(2,1)} %copies.1), calls=%async_computation | async-start | bytes 786432 | tf_op jit(solution)/shard_map/all_to_all | solution.py:257
  29.2 4.8 %copy-start = (s32[512]{0:T(512)S(1)}, s32[512]{0:T(512)}, u32[]{:S(2)}) copy-start(s32[512]{0:T(512)} %aggregate_far.1) | copy-start | bytes 6148
  29.3 6.6 %collective-permute-start.3 = (bf16[4,800,128]{2,1,0:T(8,128)(2,1)S(1)}, bf16[4,800,128]{2,1,0:T(8,128)(2,1)S(1)}, u32[]{:S(2)}, u32[]{:S(2)}) collective-permute-start(bf16[4,800,128]{2,1,0:T(8,128)(2,1)S(1)} %fusion.3), channel_id=1, source_target_pairs={{0,1},{1,0},{2,3},{3,2},{4,5},{5,4},{6,7},{7,6},{8,9},{9,8},{10,11... | collective-permute-start | bytes 2457608 | tf_op jit(solution)/shard_map/ppermute | solution.py:229
  35.9 2.8 %collective-permute-start.6 = (bf16[800,128]{1,0:T(8,128)(2,1)S(1)}, bf16[800,128]{1,0:T(8,128)(2,1)S(1)}, u32[]{:S(2)}, u32[]{:S(2)}) collective-permute-start(bf16[800,128]{1,0:T(8,128)(2,1)S(1)} %copy-done.1), channel_id=1, source_target_pairs={{192,210},{193,211},{194,208},{195,209},{196,214},{197,215},{198,2... | collective-permute-start | bytes 614408 | tf_op jit(solution)/shard_map/ppermute | solution.py:229
  36.6 2.1 %collective-permute-start.5 = (bf16[800,128]{1,0:T(8,128)(2,1)S(1)}, bf16[800,128]{1,0:T(8,128)(2,1)S(1)}, u32[]{:S(2)}, u32[]{:S(2)}) collective-permute-start(bf16[800,128]{1,0:T(8,128)(2,1)S(1)} %copy-done.1), channel_id=1, source_target_pairs={{128,144},{129,145},{130,146},{131,147},{132,148},{133,149},{134,1... | collective-permute-start | bytes 614408 | tf_op jit(solution)/shard_map/ppermute | solution.py:229
  37.3 1.4 %collective-permute-start.4 = (bf16[800,128]{1,0:T(8,128)(2,1)S(1)}, bf16[800,128]{1,0:T(8,128)(2,1)S(1)}, u32[]{:S(2)}, u32[]{:S(2)}) collective-permute-start(bf16[800,128]{1,0:T(8,128)(2,1)S(1)} %copy-done.1), channel_id=1, source_target_pairs={{128,130},{129,131},{130,128},{131,129},{132,134},{133,135},{134,1... | collective-permute-start | bytes 614408 | tf_op jit(solution)/shard_map/ppermute | solution.py:229
  38.9 0.7 collective-permute-start.8

commit v5 on v4

--- a/solution.py
+++ b/solution.py
@@ -148,20 +148,24 @@
 def place_kernel(parts, out, wide):
     yh, zl = lax.axis_index("yh"), lax.axis_index("zl")
     row = yh * 8 + lax.axis_index("zh") * 2 + zl
-    lane = lax.broadcasted_iota(jnp.int32, (PAIR, 384), 1)
+    lane = lax.broadcasted_iota(jnp.int32, (PAIR, 256), 1)
     wide[:, : 6 * 128] = jnp.zeros((PAIR, 6 * 128), jnp.float32)
     wide[:, 18 * 128 :] = jnp.zeros((PAIR, 7 * 128), jnp.float32)
     for ahead in range(4):
-        block = jnp.zeros((PAIR, 384), jnp.float32)
+        windows = [jnp.zeros((PAIR, 256), jnp.float32) for _ in range(2)]
         for low in range(2):
             part = parts[member(yh, ahead) * 2 + (low ^ zl)]
             rest = part[PAIR:, :]
             tail = jnp.concatenate([rest, pltpu.roll(rest, 64, axis=1)], axis=0)
-            source = jnp.concatenate([part[:PAIR, :], tail, jnp.zeros_like(tail)], axis=1)
+            source = jnp.concatenate([part[:PAIR, :], tail], axis=1)
             for y in range(4):
                 start = (y * 2 + low) * PAIR
-                turned = pltpu.roll(source, (start - y * PAIR) % 384, axis=1)
-                block = jnp.where((lane >= start) & (lane < start + PAIR), turned, block)
+                w = 0 if start < 240 else 1
+                at = start - 128 * w
+                turned = pltpu.roll(source, (at - y * PAIR) % 256, axis=1)
+                windows[w] = jnp.where((lane >= at) & (lane < at + PAIR), turned, windows[w])
+        first, last = windows
+        block = jnp.concatenate([first[:, :128], first[:, 128:] + last[:, :128], last[:, 128:]], axis=1)
         at = (6 + 3 * ((yh + ahead) & 3)) * 128
         wide[:, pl.ds(pl.multiple_of(at, 128), 384)] = block
     offset = row * PAIR

time: 73.4 us -> 73.4 us (level)
  no operation moved by 1% of the time
where the time goes in v5:
time: 73.4 us; the launch traced here: 73 us
  starting transfers between devices  33.1 us (45%)
  blocking collectives  29.8 us (41%)
  Pallas kernels  7.42 us (10%)
  waiting for transfers between devices  2.04 us (3%)
    ppermute x8, starting transfers between devices, swapped(): return lax.ppermute(x, AXES, flips(groups, *names))  20.3 us
    all_to_all x1, blocking collectives, local(): lax.all_to_all(jnp.broadcast_to(whole[None], (8,) + whole.shape), SHARE,...  15 us
    all_to_all x1, blocking collectives, local(): shares = lax.all_to_all(part, 'xh', 0, 0, tiled=True)  14.8 us
    all_to_all x1, starting transfers between devices, local(): gathered = lax.all_to_all(copies, 'zh', 0, 0, tiled=True)  7.13 us
    ppermute x1, starting transfers between devices, local(): turned = lax.ppermute(panels, AXES, pairs)  5.73 us
    pallas_call x1, Pallas kernels, local(): pl.pallas_call(left_kernel, out_shape=jax.ShapeDtypeStruct((PLANES * SLOT...  2.53 us
    pallas_call x1, Pallas kernels, local(): pl.pallas_call(middle_kernel, out_shape=jax.ShapeDtypeStruct((4, PAIR + M...  1.77 us
    pallas_call x1, Pallas kernels, local(): pl.pallas_call(place_kernel, out_shape=jax.ShapeDtypeStruct((AGG_DEV, MOD...  1.68 us
  transfers between devices with their start and end apart: 10, of which 2 were waited for; matrix products, arithmetic and copies ran while one was open for 0% of the time, Pallas kernels for 5%

profile of v5, /device:TPU:1, one launch (start us, length us, event | category | flops | bytes accessed | tf_op | source)
XLA Modules:
  0.0 73.0 jit_solution(4052887245964243311)
XLA Ops:
  0.0 5.7 %collective-permute-start.7 = (bf16[16,24,128]{2,1,0:T(8,128)(2,1)}, bf16[16,24,128]{2,1,0:T(8,128)(2,1)S(1)}, u32[]{:S(2)}, u32[]{:S(2)}) collective-permute-start(bf16[16,24,128]{2,1,0:T(8,128)(2,1)} %refs_4_.1), channel_id=1, source_target_pairs={{0,0},{33,1},{786,2},{819,3},{4,4},{37,5},{790,6},{823,7},{8,8},{4... | collective-permute-start | bytes 294920 | tf_op jit(solution)/shard_map/ppermute | solution.py:204
  5.7 2.5 %left.1 = bf16[800,128]{1,0:T(8,128)(2,1)} custom-call(bf16[16,2,128,128]{3,2,1,0:T(8,128)(2,1)} %refs_0_.1, s32[2,16]{1,0:T(2,128)} %bitcast.17, s32[1,16]{1,0:T(1,128)} %bitcast.18, s32[512]{0:T(512)} %aggregate_far.1, bf16[16,24,128]{2,1,0:T(8,128)(2,1)} %refs_4_.1), custom_call_target="tpu_custom_call" | custom-call | flops 25000000 | bytes 2000000 | tf_op jit(solution)/shard_map/left/pallas_call | solution.py:206
  8.3 5.4 %collective-permute-start.2 = (bf16[800,128]{1,0:T(8,128)(2,1)}, bf16[800,128]{1,0:T(8,128)(2,1)S(1)}, u32[]{:S(2)}, u32[]{:S(2)}) collective-permute-start(bf16[800,128]{1,0:T(8,128)(2,1)} %left.1), channel_id=1, source_target_pairs={{0,18},{1,19},{2,16},{3,17},{4,22},{5,23},{6,20},{7,21},{8,26},{9,... | collective-permute-start | bytes 614408 | tf_op jit(solution)/shard_map/ppermute | solution.py:233
  13.7 4.5 %collective-permute-start.1 = (bf16[800,128]{1,0:T(8,128)(2,1)}, bf16[800,128]{1,0:T(8,128)(2,1)S(1)}, u32[]{:S(2)}, u32[]{:S(2)}) collective-permute-start(bf16[800,128]{1,0:T(8,128)(2,1)} %left.1), channel_id=1, source_target_pairs={{0,16},{1,17},{2,18},{3,19},{4,20},{5,21},{6,22},{7,23},{8,24},{9,... | collective-permute-start | bytes 614408 | tf_op jit(solution)/shard_map/ppermute | solution.py:233
  18.2 3.0 %collective-permute-start = (bf16[800,128]{1,0:T(8,128)(2,1)}, bf16[800,128]{1,0:T(8,128)(2,1)S(1)}, u32[]{:S(2)}, u32[]{:S(2)}) collective-permute-start(bf16[800,128]{1,0:T(8,128)(2,1)} %left.1), channel_id=1, source_target_pairs={{0,2},{1,3},{2,0},{3,1},{4,6},{5,7},{6,4},{7,5},{8,10},{9,11},{10,... | collective-permute-start | bytes 614408 | tf_op jit(solution)/shard_map/ppermute | solution.py:233
  21.2 0.0 collective-permute-done.7.one
  21.2 0.8 %copies.1 = bf16[4,16,24,128]{3,2,1,0:T(8,128)(2,1)} custom-call(bf16[16,24,128]{2,1,0:T(8,128)(2,1)S(1)} %collective-permute-done.7.one), custom_call_target="tpu_custom_call" | custom-call | flops 99999997952 | bytes 500000 | tf_op jit(solution)/shard_map/copies/pallas_call | solution.py:251
  22.0 0.0 copy-start.1
  22.0 7.1 %all-to-all-start = ((bf16[4,16,24,128]{3,2,1,0:T(8,128)(2,1)}), bf16[4,16,24,128]{3,2,1,0:T(8,128)(2,1)S(1)}, u32[]{:S(2)}, u32[]{:S(2)}) async-start(bf16[4,16,24,128]{3,2,1,0:T(8,128)(2,1)} %copies.1), calls=%async_computation | async-start | bytes 786432 | tf_op jit(solution)/shard_map/all_to_all | solution.py:261
  29.2 0.0 collective-permute-done.2
  29.2 0.0 collective-permute-done.1
  29.2 0.0 collective-permute-done
  29.2 0.0 copy-done.1
  29.2 0.0 copy-start
  29.2 0.1 fusion.3
  29.3 4.6 %collective-permute-start.3 = (bf16[4,800,128]{2,1,0:T(8,128)(2,1)S(1)}, bf16[4,800,128]{2,1,0:T(8,128)(2,1)S(1)}, u32[]{:S(2)}, u32[]{:S(2)}) collective-permute-start(bf16[4,800,128]{2,1,0:T(8,128)(2,1)S(1)} %fusion.3), channel_id=1, source_target_pairs={{0,1},{1,0},{2,3},{3,2},{4,5},{5,4},{6,7},{7,6},{8,9},{9,8},{10,11... | collective-permute-start | bytes 2457608 | tf_op jit(solution)/shard_map/ppermute | solution.py:233
  34.0 0.0 copy-done
  34.0 0.7 halves.1.which
  34.6 1.3 %collective-permute-done.3.far = bf16[4,800,128]{2,1,0:T(8,128)(2,1)S(1)} collective-permute-done((bf16[4,800,128]{2,1,0:T(8,128)(2,1)S(1)}, bf16[4,800,128]{2,1,0:T(8,128)(2,1)S(1)}, u32[]{:S(2)}, u32[]{:S(2)}) %collective-permute-start.3) | collective-permute-done | bytes 819232 | tf_op jit(solution)/shard_map/ppermute | solution.py:233
  35.9 0.7 collective-permute-start.6
  36.6 0.7 collective-permute-start.5
  37.3 0.7 collective-permute-start.4
  37.9 0.8 %all-to-all-done.panels = bf16[4,16,24,128]{3,2,1,0:T(8,128)(2,1)S(1)} async-done(((bf16[4,16,24,128]{3,2,1,0:T(8,128)(2,1)}), bf16[4,16,24,128]{3,2,1,0:T(8,128)(2,1)S(1)}, u32[]{:S(2)}, u32[]{:S(2)}) %all-to-all-start) | async-done | bytes 393248 | tf_op jit(solution)/shard_map/all_to_all | solution.py:261
  38.7 0.0 collective-permute-done.6
  38.7 0.0 collective-permute-done.5
  38.7 0.0 collective-permute-done.4
  38.7 0.1 add_bitcast_fusion
  38.8 0.1 fusion.1.near
  38.9 0.7 collective-permute-start.8
  39.6 0.0 collective-permute-done.8.far_late
  39.6 1.8 %middle.1 = f32[4,72,128]{2,1,0:T(8,128)S(1)} custom-call(bf16[4,800,128]{2,1,0:T(8,128)(2,1)S(1)} %fusion.1.near, bf16[4,800,128]{2,1,0:T(8,128)(2,1)S(1)} %collective-permute-done.3.far, bf16[4,800,128]{2,1,0:T(8,128)(2,1)S(1)} %collective-permute-done.8.far_late, bf16[4,16,24,128]{3,2,1,0:T(8,128)(2,1)S(1)} %all-to-all-done.panels, f32[64,128]{1,0:T(8,128)S(1)} %halves.1.which), custom_call_target="tpu_custom_call" | custom-call | flops 500000000 | bytes 3000000 | tf_op jit(solution)/shard_map/middle/pallas_call | solution.py:269
  41.4 14.8 %all_to_all.15 = f32[4,72,128]{2,1,0:T(8,128)S(1)} all-to-all(f32[4,72,128]{2,1,0:T(8,128)S(1)} %middle.1), channel_id=1, replica_groups=mesh['yh'=4,'zh'=4,'zl'=2,'yl'=2,'xh'=4,'xl'=2,'k'=2] {'xh'}, dimensions={0} | all-to-all | bytes 294912 | tf_op jit(solution)/shard_map/all_to_all | solution.py:286
  56.3 15.0 %all_to_all.16.parts = f32[8,72,128]{2,1,0:T(8,128)S(1)} all-to-all(f32[8,72,128]{2,1,0:T(8,128)S(1)} %broadcast_in_dim.2), channel_id=1, replica_groups=mesh['yh'=4,'zh'=4,'zl'=2,'yl'=2,'xh'=4,'xl'=2,'k'=2] {'yl','xl','k'}, dimensions={0} | all-to-all | bytes 589824 | tf_op jit(solution)/shard_map/all_to_all | solution.py:288
  71.3 1.7 %place.1 = f32[2,24,1584]{2,1,0:T(8,128)} custom-call(f32[8,72,128]{2,1,0:T(8,128)S(1)} %all_to_all.16.parts), custom_call_target="tpu_custom_call" | custom-call | flops 1000000 | bytes 600000 | tf_op jit(solution)/shard_map/place/pallas_call | solution.py:291
  (3 shorter events, 0.1 us)
Async XLA Ops:
  0.0 21.2 %collective-permute-start.7 = (bf16[16,24,128]{2,1,0:T(8,128)(2,1)}, bf16[16,24,128]{2,1,0:T(8,128)(2,1)S(1)}, u32[]{:S(2)}, u32[]{:S(2)}) collective-permute-start(bf16[16,24,128]{2,1,0:T(8,128)(2,1)} %refs_4_.1), channel_id=1, source_target_pairs={{0,0},{33,1},{786,2},{819,3},{4,4},{37,5},{790,6},{823,7},{8,8},{4... | collective-permute-start | bytes 294920 | tf_op jit(solution)/shard_map/ppermute | solution.py:204
  8.3 20.9 %collective-permute-start.2 = (bf16[800,128]{1,0:T(8,128)(2,1)}, bf16[800,128]{1,0:T(8,128)(2,1)S(1)}, u32[]{:S(2)}, u32[]{:S(2)}) collective-permute-start(bf16[800,128]{1,0:T(8,128)(2,1)} %left.1), channel_id=1, source_target_pairs={{0,18},{1,19},{2,16},{3,17},{4,22},{5,23},{6,20},{7,21},{8,26},{9,... | collective-permute-start | bytes 614408 | tf_op jit(solution)/shard_map/ppermute | solution.py:233
  13.7 15.5 %collective-permute-start.1 = (bf16[800,128]{1,0:T(8,128)(2,1)}, bf16[800,128]{1,0:T(8,128)(2,1)S(1)}, u32[]{:S(2)}, u32[]{:S(2)}) collective-permute-start(bf16[800,128]{1,0:T(8,128)(2,1)} %left.1), channel_id=1, source_target_pairs={{0,16},{1,17},{2,18},{3,19},{4,20},{5,21},{6,22},{7,23},{8,24},{9,... | collective-permute-start | bytes 614408 | tf_op jit(solution)/shard_map/ppermute | solution.py:233
  18.2 11.0 %collective-permute-start = (bf16[800,128]{1,0:T(8,128)(2,1)}, bf16[800,128]{1,0:T(8,128)(2,1)S(1)}, u32[]{:S(2)}, u32[]{:S(2)}) collective-permute-start(bf16[800,128]{1,0:T(8,128)(2,1)} %left.1), channel_id=1, source_target_pairs={{0,2},{1,3},{2,0},{3,1},{4,6},{5,7},{6,4},{7,5},{8,10},{9,11},{10,... | collective-permute-start | bytes 614408 | tf_op jit(solution)/shard_map/ppermute | solution.py:233
  22.0 7.2 %copy-start.1 = (bf16[800,128]{1,0:T(8,128)(2,1)S(1)}, bf16[800,128]{1,0:T(8,128)(2,1)}, u32[]{:S(2)}) copy-start(bf16[800,128]{1,0:T(8,128)(2,1)} %left.1) | copy-start | bytes 614404
  22.0 16.7 %all-to-all-start = ((bf16[4,16,24,128]{3,2,1,0:T(8,128)(2,1)}), bf16[4,16,24,128]{3,2,1,0:T(8,128)(2,1)S(1)}, u32[]{:S(2)}, u32[]{:S(2)}) async-start(bf16[4,16,24,128]{3,2,1,0:T(8,128)(2,1)} %copies.1), calls=%async_computation | async-start | bytes 786432 | tf_op jit(solution)/shard_map/all_to_all | solution.py:261
  29.2 4.8 %copy-start = (s32[512]{0:T(512)S(1)}, s32[512]{0:T(512)}, u32[]{:S(2)}) copy-start(s32[512]{0:T(512)} %aggregate_far.1) | copy-start | bytes 6148
  29.3 6.6 %collective-permute-start.3 = (bf16[4,800,128]{2,1,0:T(8,128)(2,1)S(1)}, bf16[4,800,128]{2,1,0:T(8,128)(2,1)S(1)}, u32[]{:S(2)}, u32[]{:S(2)}) collective-permute-start(bf16[4,800,128]{2,1,0:T(8,128)(2,1)S(1)} %fusion.3), channel_id=1, source_target_pairs={{0,1},{1,0},{2,3},{3,2},{4,5},{5,4},{6,7},{7,6},{8,9},{9,8},{10,11... | collective-permute-start | bytes 2457608 | tf_op jit(solution)/shard_map/ppermute | solution.py:233
  35.9 2.8 %collective-permute-start.6 = (bf16[800,128]{1,0:T(8,128)(2,1)S(1)}, bf16[800,128]{1,0:T(8,128)(2,1)S(1)}, u32[]{:S(2)}, u32[]{:S(2)}) collective-permute-start(bf16[800,128]{1,0:T(8,128)(2,1)S(1)} %copy-done.1), channel_id=1, source_target_pairs={{192,210},{193,211},{194,208},{195,209},{196,214},{197,215},{198,2... | collective-permute-start | bytes 614408 | tf_op jit(solution)/shard_map/ppermute | solution.py:233
  36.6 2.1 %collective-permute-start.5 = (bf16[800,128]{1,0:T(8,128)(2,1)S(1)}, bf16[800,128]{1,0:T(8,128)(2,1)S(1)}, u32[]{:S(2)}, u32[]{:S(2)}) collective-permute-start(bf16[800,128]{1,0:T(8,128)(2,1)S(1)} %copy-done.1), channel_id=1, source_target_pairs={{128,144},{129,145},{130,146},{131,147},{132,148},{133,149},{134,1... | collective-permute-start | bytes 614408 | tf_op jit(solution)/shard_map/ppermute | solution.py:233
  37.3 1.4 %collective-permute-start.4 = (bf16[800,128]{1,0:T(8,128)(2,1)S(1)}, bf16[800,128]{1,0:T(8,128)(2,1)S(1)}, u32[]{:S(2)}, u32[]{:S(2)}) collective-permute-start(bf16[800,128]{1,0:T(8,128)(2,1)S(1)} %copy-done.1), channel_id=1, source_target_pairs={{128,130},{129,131},{130,128},{131,129},{132,134},{133,135},{134,1... | collective-permute-start | bytes 614408 | tf_op jit(solution)/shard_map/ppermute | solution.py:233
  38.9 0.7 collective-permute-start.8

commit v6 on v5

--- a/solution.py
+++ b/solution.py
@@ -145,7 +145,7 @@
         out[u, PAIR:, :] = rest
 
 
-def place_kernel(parts, out, wide):
+def place_kernel(parts, out, wide, held, sent):
     yh, zl = lax.axis_index("yh"), lax.axis_index("zl")
     row = yh * 8 + lax.axis_index("zh") * 2 + zl
     lane = lax.broadcasted_iota(jnp.int32, (PAIR, 256), 1)
@@ -171,16 +171,22 @@
     offset = row * PAIR
     base = pl.multiple_of((offset // 128) * 128, 128)
     shift = offset % 128
-    narrow = lax.broadcasted_iota(jnp.int32, (PAIR, 128), 1)
-    turned = []
-    for t in range(14):
-        tile = wide[:, pl.ds(base + t * 128, 128)]
-        turned.append(pltpu.roll(tile, (128 - shift) % 128, axis=1))
-    for t in range(13):
-        tile = jnp.where(narrow < 128 - shift, turned[t], turned[t + 1])
-        width = min(128, WIN - t * 128)
-        for a in range(AGG_DEV):
-            out[a, :, t * 128 : t * 128 + width] = tile[a * MODES : (a + 1) * MODES, :width]
+    narrow = lax.broadcasted_iota(jnp.int32, (MODES, 128), 1)
+    copies = []
+    for a in range(AGG_DEV):
+        rows = slice(a * MODES, (a + 1) * MODES)
+        turned = []
+        for t in range(14):
+            tile = wide[rows, pl.ds(base + t * 128, 128)]
+            turned.append(pltpu.roll(tile, (128 - shift) % 128, axis=1))
+        for t in range(13):
+            tile = jnp.where(narrow < 128 - shift, turned[t], turned[t + 1])
+            width = min(128, WIN - t * 128)
+            held[a, :, t * 128 : t * 128 + width] = tile[:, :width]
+        copies.append(pltpu.make_async_copy(held.at[a], out.at[a], sent.at[a]))
+        copies[a].start()
+    for copy in copies:
+        copy.wait()
 
 
 def everything(space, count):
@@ -292,8 +298,12 @@
         place_kernel,
         out_shape=jax.ShapeDtypeStruct((AGG_DEV, MODES, WIN), f32),
         in_specs=[pl.BlockSpec(memory_space=VMEM)],
-        out_specs=pl.BlockSpec(memory_space=VMEM),
-        scratch_shapes=[pltpu.VMEM((PAIR, 25 * 128), f32)],
+        out_specs=pl.BlockSpec(memory_space=pl.ANY),
+        scratch_shapes=[
+            pltpu.VMEM((PAIR, 25 * 128), f32),
+            pltpu.VMEM((AGG_DEV, MODES, WIN), f32),
+            pltpu.SemaphoreType.DMA((AGG_DEV,)),
+        ],
         compiler_params=params,
         cost_estimate=pl.CostEstimate(flops=1_000_000, bytes_accessed=600_000, transcendentals=0),
         name="place",

time: 73.4 us -> 73.4 us (level)
  no operation moved by 1% of the time
where the time goes in v6:
time: 73.4 us; the launch traced here: 73 us
  starting transfers between devices  33.1 us (45%)
  blocking collectives  29.8 us (41%)
  Pallas kernels  7.39 us (10%)
  waiting for transfers between devices  2.04 us (3%)
    ppermute x8, starting transfers between devices, swapped(): return lax.ppermute(x, AXES, flips(groups, *names))  20.3 us
    all_to_all x1, blocking collectives, local(): lax.all_to_all(jnp.broadcast_to(whole[None], (8,) + whole.shape), SHARE,...  15 us
    all_to_all x1, blocking collectives, local(): shares = lax.all_to_all(part, 'xh', 0, 0, tiled=True)  14.8 us
    all_to_all x1, starting transfers between devices, local(): gathered = lax.all_to_all(copies, 'zh', 0, 0, tiled=True)  7.13 us
    ppermute x1, starting transfers between devices, local(): turned = lax.ppermute(panels, AXES, pairs)  5.73 us
    pallas_call x1, Pallas kernels, local(): pl.pallas_call(left_kernel, out_shape=jax.ShapeDtypeStruct((PLANES * SLOT...  2.53 us
    pallas_call x1, Pallas kernels, local(): pl.pallas_call(middle_kernel, out_shape=jax.ShapeDtypeStruct((4, PAIR + M...  1.77 us
    pallas_call x1, Pallas kernels, local(): pl.pallas_call(place_kernel, out_shape=jax.ShapeDtypeStruct((AGG_DEV, MOD...  1.65 us
  transfers between devices with their start and end apart: 10, of which 2 were waited for; matrix products, arithmetic and copies ran while one was open for 0% of the time, Pallas kernels for 5%

profile of v6, /device:TPU:1, one launch (start us, length us, event | category | flops | bytes accessed | tf_op | source)
XLA Modules:
  0.0 73.0 jit_solution(16159267561788516603)
XLA Ops:
  0.0 5.7 %collective-permute-start.7 = (bf16[16,24,128]{2,1,0:T(8,128)(2,1)}, bf16[16,24,128]{2,1,0:T(8,128)(2,1)S(1)}, u32[]{:S(2)}, u32[]{:S(2)}) collective-permute-start(bf16[16,24,128]{2,1,0:T(8,128)(2,1)} %refs_4_.1), channel_id=1, source_target_pairs={{0,0},{33,1},{786,2},{819,3},{4,4},{37,5},{790,6},{823,7},{8,8},{4... | collective-permute-start | bytes 294920 | tf_op jit(solution)/shard_map/ppermute | solution.py:210
  5.7 2.5 %left.1 = bf16[800,128]{1,0:T(8,128)(2,1)} custom-call(bf16[16,2,128,128]{3,2,1,0:T(8,128)(2,1)} %refs_0_.1, s32[2,16]{1,0:T(2,128)} %bitcast.17, s32[1,16]{1,0:T(1,128)} %bitcast.18, s32[512]{0:T(512)} %aggregate_far.1, bf16[16,24,128]{2,1,0:T(8,128)(2,1)} %refs_4_.1), custom_call_target="tpu_custom_call" | custom-call | flops 25000000 | bytes 2000000 | tf_op jit(solution)/shard_map/left/pallas_call | solution.py:212
  8.3 5.4 %collective-permute-start.2 = (bf16[800,128]{1,0:T(8,128)(2,1)}, bf16[800,128]{1,0:T(8,128)(2,1)S(1)}, u32[]{:S(2)}, u32[]{:S(2)}) collective-permute-start(bf16[800,128]{1,0:T(8,128)(2,1)} %left.1), channel_id=1, source_target_pairs={{0,18},{1,19},{2,16},{3,17},{4,22},{5,23},{6,20},{7,21},{8,26},{9,... | collective-permute-start | bytes 614408 | tf_op jit(solution)/shard_map/ppermute | solution.py:239
  13.7 4.5 %collective-permute-start.1 = (bf16[800,128]{1,0:T(8,128)(2,1)}, bf16[800,128]{1,0:T(8,128)(2,1)S(1)}, u32[]{:S(2)}, u32[]{:S(2)}) collective-permute-start(bf16[800,128]{1,0:T(8,128)(2,1)} %left.1), channel_id=1, source_target_pairs={{0,16},{1,17},{2,18},{3,19},{4,20},{5,21},{6,22},{7,23},{8,24},{9,... | collective-permute-start | bytes 614408 | tf_op jit(solution)/shard_map/ppermute | solution.py:239
  18.2 3.0 %collective-permute-start = (bf16[800,128]{1,0:T(8,128)(2,1)}, bf16[800,128]{1,0:T(8,128)(2,1)S(1)}, u32[]{:S(2)}, u32[]{:S(2)}) collective-permute-start(bf16[800,128]{1,0:T(8,128)(2,1)} %left.1), channel_id=1, source_target_pairs={{0,2},{1,3},{2,0},{3,1},{4,6},{5,7},{6,4},{7,5},{8,10},{9,11},{10,... | collective-permute-start | bytes 614408 | tf_op jit(solution)/shard_map/ppermute | solution.py:239
  21.2 0.0 collective-permute-done.7.one
  21.2 0.8 %copies.1 = bf16[4,16,24,128]{3,2,1,0:T(8,128)(2,1)} custom-call(bf16[16,24,128]{2,1,0:T(8,128)(2,1)S(1)} %collective-permute-done.7.one), custom_call_target="tpu_custom_call" | custom-call | flops 99999997952 | bytes 500000 | tf_op jit(solution)/shard_map/copies/pallas_call | solution.py:257
  22.0 0.0 copy-start.1
  22.0 7.1 %all-to-all-start = ((bf16[4,16,24,128]{3,2,1,0:T(8,128)(2,1)}), bf16[4,16,24,128]{3,2,1,0:T(8,128)(2,1)S(1)}, u32[]{:S(2)}, u32[]{:S(2)}) async-start(bf16[4,16,24,128]{3,2,1,0:T(8,128)(2,1)} %copies.1), calls=%async_computation | async-start | bytes 786432 | tf_op jit(solution)/shard_map/all_to_all | solution.py:267
  29.2 0.0 collective-permute-done.2
  29.2 0.0 collective-permute-done.1
  29.2 0.0 collective-permute-done
  29.2 0.0 copy-done.1
  29.2 0.0 copy-start
  29.2 0.1 fusion.3
  29.3 4.6 %collective-permute-start.3 = (bf16[4,800,128]{2,1,0:T(8,128)(2,1)S(1)}, bf16[4,800,128]{2,1,0:T(8,128)(2,1)S(1)}, u32[]{:S(2)}, u32[]{:S(2)}) collective-permute-start(bf16[4,800,128]{2,1,0:T(8,128)(2,1)S(1)} %fusion.3), channel_id=1, source_target_pairs={{0,1},{1,0},{2,3},{3,2},{4,5},{5,4},{6,7},{7,6},{8,9},{9,8},{10,11... | collective-permute-start | bytes 2457608 | tf_op jit(solution)/shard_map/ppermute | solution.py:239
  34.0 0.0 copy-done
  34.0 0.7 halves.1.which
  34.6 1.3 %collective-permute-done.3.far = bf16[4,800,128]{2,1,0:T(8,128)(2,1)S(1)} collective-permute-done((bf16[4,800,128]{2,1,0:T(8,128)(2,1)S(1)}, bf16[4,800,128]{2,1,0:T(8,128)(2,1)S(1)}, u32[]{:S(2)}, u32[]{:S(2)}) %collective-permute-start.3) | collective-permute-done | bytes 819232 | tf_op jit(solution)/shard_map/ppermute | solution.py:239
  35.9 0.7 collective-permute-start.6
  36.6 0.7 collective-permute-start.5
  37.3 0.7 collective-permute-start.4
  37.9 0.8 %all-to-all-done.panels = bf16[4,16,24,128]{3,2,1,0:T(8,128)(2,1)S(1)} async-done(((bf16[4,16,24,128]{3,2,1,0:T(8,128)(2,1)}), bf16[4,16,24,128]{3,2,1,0:T(8,128)(2,1)S(1)}, u32[]{:S(2)}, u32[]{:S(2)}) %all-to-all-start) | async-done | bytes 393248 | tf_op jit(solution)/shard_map/all_to_all | solution.py:267
  38.7 0.0 collective-permute-done.6
  38.7 0.0 collective-permute-done.5
  38.7 0.0 collective-permute-done.4
  38.7 0.1 add_bitcast_fusion
  38.8 0.1 fusion.1.near
  38.9 0.7 collective-permute-start.8
  39.6 0.0 collective-permute-done.8.far_late
  39.6 1.8 %middle.1 = f32[4,72,128]{2,1,0:T(8,128)S(1)} custom-call(bf16[4,800,128]{2,1,0:T(8,128)(2,1)S(1)} %fusion.1.near, bf16[4,800,128]{2,1,0:T(8,128)(2,1)S(1)} %collective-permute-done.3.far, bf16[4,800,128]{2,1,0:T(8,128)(2,1)S(1)} %collective-permute-done.8.far_late, bf16[4,16,24,128]{3,2,1,0:T(8,128)(2,1)S(1)} %all-to-all-done.panels, f32[64,128]{1,0:T(8,128)S(1)} %halves.1.which), custom_call_target="tpu_custom_call" | custom-call | flops 500000000 | bytes 3000000 | tf_op jit(solution)/shard_map/middle/pallas_call | solution.py:275
  41.4 14.8 %all_to_all.15 = f32[4,72,128]{2,1,0:T(8,128)S(1)} all-to-all(f32[4,72,128]{2,1,0:T(8,128)S(1)} %middle.1), channel_id=1, replica_groups=mesh['yh'=4,'zh'=4,'zl'=2,'yl'=2,'xh'=4,'xl'=2,'k'=2] {'xh'}, dimensions={0} | all-to-all | bytes 294912 | tf_op jit(solution)/shard_map/all_to_all | solution.py:292
  56.3 15.0 %all_to_all.16.parts = f32[8,72,128]{2,1,0:T(8,128)S(1)} all-to-all(f32[8,72,128]{2,1,0:T(8,128)S(1)} %broadcast_in_dim.2), channel_id=1, replica_groups=mesh['yh'=4,'zh'=4,'zl'=2,'yl'=2,'xh'=4,'xl'=2,'k'=2] {'yl','xl','k'}, dimensions={0} | all-to-all | bytes 589824 | tf_op jit(solution)/shard_map/all_to_all | solution.py:294
  71.3 1.7 %place.1 = f32[2,24,1584]{2,1,0:T(8,128)} custom-call(f32[8,72,128]{2,1,0:T(8,128)S(1)} %all_to_all.16.parts), custom_call_target="tpu_custom_call" | custom-call | flops 1000000 | bytes 600000 | tf_op jit(solution)/shard_map/place/pallas_call | solution.py:297
  (3 shorter events, 0.1 us)
Async XLA Ops:
  0.0 21.2 %collective-permute-start.7 = (bf16[16,24,128]{2,1,0:T(8,128)(2,1)}, bf16[16,24,128]{2,1,0:T(8,128)(2,1)S(1)}, u32[]{:S(2)}, u32[]{:S(2)}) collective-permute-start(bf16[16,24,128]{2,1,0:T(8,128)(2,1)} %refs_4_.1), channel_id=1, source_target_pairs={{0,0},{33,1},{786,2},{819,3},{4,4},{37,5},{790,6},{823,7},{8,8},{4... | collective-permute-start | bytes 294920 | tf_op jit(solution)/shard_map/ppermute | solution.py:210
  8.3 20.9 %collective-permute-start.2 = (bf16[800,128]{1,0:T(8,128)(2,1)}, bf16[800,128]{1,0:T(8,128)(2,1)S(1)}, u32[]{:S(2)}, u32[]{:S(2)}) collective-permute-start(bf16[800,128]{1,0:T(8,128)(2,1)} %left.1), channel_id=1, source_target_pairs={{0,18},{1,19},{2,16},{3,17},{4,22},{5,23},{6,20},{7,21},{8,26},{9,... | collective-permute-start | bytes 614408 | tf_op jit(solution)/shard_map/ppermute | solution.py:239
  13.7 15.5 %collective-permute-start.1 = (bf16[800,128]{1,0:T(8,128)(2,1)}, bf16[800,128]{1,0:T(8,128)(2,1)S(1)}, u32[]{:S(2)}, u32[]{:S(2)}) collective-permute-start(bf16[800,128]{1,0:T(8,128)(2,1)} %left.1), channel_id=1, source_target_pairs={{0,16},{1,17},{2,18},{3,19},{4,20},{5,21},{6,22},{7,23},{8,24},{9,... | collective-permute-start | bytes 614408 | tf_op jit(solution)/shard_map/ppermute | solution.py:239
  18.2 11.0 %collective-permute-start = (bf16[800,128]{1,0:T(8,128)(2,1)}, bf16[800,128]{1,0:T(8,128)(2,1)S(1)}, u32[]{:S(2)}, u32[]{:S(2)}) collective-permute-start(bf16[800,128]{1,0:T(8,128)(2,1)} %left.1), channel_id=1, source_target_pairs={{0,2},{1,3},{2,0},{3,1},{4,6},{5,7},{6,4},{7,5},{8,10},{9,11},{10,... | collective-permute-start | bytes 614408 | tf_op jit(solution)/shard_map/ppermute | solution.py:239
  22.0 7.2 %copy-start.1 = (bf16[800,128]{1,0:T(8,128)(2,1)S(1)}, bf16[800,128]{1,0:T(8,128)(2,1)}, u32[]{:S(2)}) copy-start(bf16[800,128]{1,0:T(8,128)(2,1)} %left.1) | copy-start | bytes 614404
  22.0 16.7 %all-to-all-start = ((bf16[4,16,24,128]{3,2,1,0:T(8,128)(2,1)}), bf16[4,16,24,128]{3,2,1,0:T(8,128)(2,1)S(1)}, u32[]{:S(2)}, u32[]{:S(2)}) async-start(bf16[4,16,24,128]{3,2,1,0:T(8,128)(2,1)} %copies.1), calls=%async_computation | async-start | bytes 786432 | tf_op jit(solution)/shard_map/all_to_all | solution.py:267
  29.2 4.8 %copy-start = (s32[512]{0:T(512)S(1)}, s32[512]{0:T(512)}, u32[]{:S(2)}) copy-start(s32[512]{0:T(512)} %aggregate_far.1) | copy-start | bytes 6148
  29.3 6.6 %collective-permute-start.3 = (bf16[4,800,128]{2,1,0:T(8,128)(2,1)S(1)}, bf16[4,800,128]{2,1,0:T(8,128)(2,1)S(1)}, u32[]{:S(2)}, u32[]{:S(2)}) collective-permute-start(bf16[4,800,128]{2,1,0:T(8,128)(2,1)S(1)} %fusion.3), channel_id=1, source_target_pairs={{0,1},{1,0},{2,3},{3,2},{4,5},{5,4},{6,7},{7,6},{8,9},{9,8},{10,11... | collective-permute-start | bytes 2457608 | tf_op jit(solution)/shard_map/ppermute | solution.py:239
  35.9 2.8 %collective-permute-start.6 = (bf16[800,128]{1,0:T(8,128)(2,1)S(1)}, bf16[800,128]{1,0:T(8,128)(2,1)S(1)}, u32[]{:S(2)}, u32[]{:S(2)}) collective-permute-start(bf16[800,128]{1,0:T(8,128)(2,1)S(1)} %copy-done.1), channel_id=1, source_target_pairs={{192,210},{193,211},{194,208},{195,209},{196,214},{197,215},{198,2... | collective-permute-start | bytes 614408 | tf_op jit(solution)/shard_map/ppermute | solution.py:239
  36.6 2.1 %collective-permute-start.5 = (bf16[800,128]{1,0:T(8,128)(2,1)S(1)}, bf16[800,128]{1,0:T(8,128)(2,1)S(1)}, u32[]{:S(2)}, u32[]{:S(2)}) collective-permute-start(bf16[800,128]{1,0:T(8,128)(2,1)S(1)} %copy-done.1), channel_id=1, source_target_pairs={{128,144},{129,145},{130,146},{131,147},{132,148},{133,149},{134,1... | collective-permute-start | bytes 614408 | tf_op jit(solution)/shard_map/ppermute | solution.py:239
  37.3 1.4 %collective-permute-start.4 = (bf16[800,128]{1,0:T(8,128)(2,1)S(1)}, bf16[800,128]{1,0:T(8,128)(2,1)S(1)}, u32[]{:S(2)}, u32[]{:S(2)}) collective-permute-start(bf16[800,128]{1,0:T(8,128)(2,1)S(1)} %copy-done.1), channel_id=1, source_target_pairs={{128,130},{129,131},{130,128},{131,129},{132,134},{133,135},{134,1... | collective-permute-start | bytes 614408 | tf_op jit(solution)/shard_map/ppermute | solution.py:239
  38.9 0.7 collective-permute-start.8
